TPU v7x, 256 devices: a whole 4x4x8 slice. The times are simulated.
256 devices in a mesh: dp: 64 (over z, x, y_lo), tensor: 4 (over y_hi, core).
Axes of the slice: x: 4, y: 4 (y_hi: 2, y_lo: 2; y = y_hi * 2 + y_lo), z: 8, core: 2. Of those that a mesh axis runs over, the one named last changes fastest.
Arguments:
- activations: bfloat16 [49152, 5120], P('dp', 'tensor'), may hold values from -6 to 6
- output_gradient: bfloat16 [49152, 5120], P(('dp', 'tensor')), may hold values from -6 to 6
- shrinking_entries: bfloat16 [5120, 128], P('tensor'), may hold values from -0.078125 to 0.078125
- expanding_entries: bfloat16 [128, 5120], replicated, may hold values from -0.5 to 0.5
- expanding_sketch: float32 [128, 32], replicated, may hold values from -0.5 to 0.5
- input_side_matrix: bfloat16 [5120, 32], P('tensor'), may hold values from -0.078125 to 0.078125
- output_side_matrix: bfloat16 [5120, 128], replicated, may hold values from -0.078125 to 0.078125
- shrinking_sketch: bfloat16 [128, 128], replicated, may hold values from -0.5 to 0.5
- heldout_gradient: bfloat16 [4096, 8192], P('dp', 'tensor'), may hold values from -6 to 6
Outputs:
- scores: float32 [384, 4096], P('dp')
- train_grads: bfloat16 [384, 8192], P('dp', 'tensor')
All inputs are finite; a program needn't handle non-finite values.
Results may differ from a plain program's by a relative error of at most 0.0058.
Values may be sent and summed in bfloat16 or wider, within the bound.
No kernel may reach another device: no remote copies, remote signals or barrier semaphores. Data moves between devices by JAX's collectives and lax.ppermute only.
A program may use at most 64 MiB of HBM per device.

v0:
```python
import math

import jax
import jax.numpy as jnp
from jax import lax
from jax.sharding import PartitionSpec as P

SEQ = 128
PROJ = 8192


def output_projector(gradient_list, expanding_entries, output_side_matrix, shrinking_sketch):
    first_factor = jnp.dot(
        gradient_list, output_side_matrix, preferred_element_type=jnp.float32
    ).astype(jnp.bfloat16)
    backward_pass = lax.dot_general(
        gradient_list,
        expanding_entries,
        (((1,), (1,)), ((), ())),
        preferred_element_type=jnp.float32,
    ).astype(jnp.bfloat16)
    second_factor = jnp.dot(
        backward_pass, shrinking_sketch, preferred_element_type=jnp.float32
    ).astype(jnp.bfloat16)
    return (first_factor, second_factor)


def outer_mean(left, right, count):
    left3 = left.reshape(count, SEQ, left.shape[1])
    right3 = right.astype(jnp.float32).reshape(count, SEQ, right.shape[1])
    prod = jnp.einsum("esk,esm->ekm", left3, right3, precision=lax.Precision.HIGHEST)
    return prod.reshape(count, -1) / SEQ


def on_device(
    activations,
    output_gradient,
    shrinking_entries,
    expanding_entries,
    expanding_sketch,
    input_side_matrix,
    output_side_matrix,
    shrinking_sketch,
    heldout_gradient,
):
    count = activations.shape[0] // SEQ
    complete_gradient = lax.all_gather(output_gradient, "tensor", axis=0, tiled=True)
    first_factor, second_factor = output_projector(
        complete_gradient, expanding_entries, output_side_matrix, shrinking_sketch
    )
    reduced_rank = jnp.dot(activations, shrinking_entries, preferred_element_type=jnp.float32)
    side_a = jnp.dot(
        reduced_rank,
        expanding_sketch,
        precision=lax.Precision.HIGHEST,
        preferred_element_type=jnp.float32,
    )
    side_c = jnp.dot(activations, input_side_matrix, preferred_element_type=jnp.float32)
    partial_grads = jnp.concatenate(
        [outer_mean(side_a, first_factor, count), outer_mean(side_c, second_factor, count)], axis=1
    )
    train_grads = lax.psum_scatter(partial_grads, "tensor", scatter_dimension=1, tiled=True).astype(
        jnp.bfloat16
    )
    train_f = train_grads.astype(jnp.float32)
    train_sq = jnp.sum(train_f * train_f, axis=1)
    scale_all = math.sqrt(PROJ)
    val_f = heldout_gradient.astype(jnp.float32)
    local_sq = jnp.sum(val_f * val_f, axis=1)
    block = lax.dot_general(
        lax.all_gather(train_grads, "dp", axis=0, tiled=True),
        heldout_gradient,
        (((1,), (1,)), ((), ())),
        preferred_element_type=jnp.float32,
    )
    columns = block
    columns, val_sq, train_total = lax.psum((columns, local_sq, train_sq), "tensor")
    scaled = columns * lax.rsqrt(val_sq + 1e-06)[None, :]
    placed = lax.all_to_all(scaled, "dp", split_axis=0, concat_axis=1, tiled=True)
    scores = placed * lax.rsqrt(train_total + 1e-06)[:, None] * scale_all
    return (scores, train_grads)


def solution(mesh):
    return jax.shard_map(
        on_device,
        mesh=mesh,
        in_specs=(
            P("dp", "tensor"),
            P(("dp", "tensor"), None),
            P("tensor", None),
            P(),
            P(),
            P("tensor", None),
            P(),
            P(),
            P("dp", "tensor"),
        ),
        out_specs=(P("dp", None), P("dp", "tensor")),
        check_vma=False,
    )
```

profile of v0, /device:TPU:1, one launch (start us, length us, event | category | flops | bytes accessed | tf_op | source)
XLA Modules:
  0.0 501.1 jit_solution(5758015474926205732)
XLA Ops:
  7.2 0.0 copy-start
  7.2 0.0 copy-start.2
  7.2 0.0 copy-start.4
  7.2 0.0 all-gather.4.cloned.1.call-start
  7.2 0.7 all-gather.4.cloned.1.call-update
  7.9 0.0 copy-start.3
  7.9 0.0 reduce-scatter.2.cloned.1.call-start
  8.0 0.7 copy-done
  8.7 0.0 copy-done.2
  8.7 0.7 fusion.6
  9.4 0.0 copy-done.4
  9.4 0.0 copy-start.5
  9.4 0.5 convolution_bitcast_fusion.1
  9.9 0.0 copy-done.3
  9.9 0.7 convolution_bitcast_fusion
  10.6 65.5 %all-gather.4.cloned.1.call-done = bf16[768,5120]{1,0:T(8,128)(2,1)} async-done(((bf16[192,5120]{1,0:T(8,128)(2,1)}), bf16[768,5120]{1,0:T(8,128)(2,1)}) %all-gather.4.cloned.1.call-update) | async-done | bytes 7864336 | tf_op jit(solution)/shard_map/all_gather | solution.py:47
  76.1 0.0 copy-done.5
  76.1 5.9 %convolution_convert_fusion = bf16[768,128]{1,0:T(8,128)(2,1)S(1)} fusion(bf16[128,128]{1,0:T(8,128)(2,1)S(1)} %copy-done.5, bf16[768,5120]{1,0:T(8,128)(2,1)} %all-gather.4.cloned.1.call-done, bf16[128,5120]{1,0:T(8,128)(2,1)} %param.12), kind=kOutput, calls=%fused_computation | convolution fusion | flops 1031995392 | bytes 9404416 | tf_op jit(solution)/shard_map/dot_general | solution.py:22
  82.0 0.3 fusion
  82.3 5.7 %convolution_convert_fusion.2 = bf16[768,128]{1,0:T(8,128)(2,1)S(1)} fusion(bf16[768,5120]{1,0:T(8,128)(2,1)} %all-gather.4.cloned.1.call-done, bf16[5120,128]{1,0:T(8,128)(2,1)} %param.15), kind=kOutput, calls=%fused_computation.2 | convolution fusion | flops 1006731264 | bytes 9371648 | tf_op jit(solution)/shard_map/dot_general | solution.py:13
  88.0 0.0 copy-start.1
  88.0 0.3 fusion.1
  88.3 0.1 copy_bitcast_fusion
  88.4 0.7 pad_maximum_fusion
  89.2 0.0 reduce-scatter.2.cloned.1.call-update
  89.2 0.0 all-gather.6.cloned.1.call-start
  89.2 31.2 %reduce-scatter.2.cloned.1.call-done = f32[6,2048]{1,0:T(8,128)} async-done(((f32[6,8192]{1,0:T(8,128)}), f32[6,2048]{1,0:T(8,128)}) %reduce-scatter.2.cloned.1.call-update) | async-done | bytes 49168 | tf_op jit(solution)/shard_map/reduce_scatter | solution.py:62
  120.4 1.6 multiply_reduce_fusion.1
  122.0 0.0 all-gather.6.cloned.1.call-update
  122.0 0.0 all-reduce.3.cloned.1.call-start
  122.0 0.0 copy-done.1
  122.1 0.2 multiply_reduce_fusion
  122.2 7.3 %all-reduce = (f32[64]{0:T(128)S(1)}, f32[6]{0:T(128)S(1)}) all-reduce(f32[64]{0:T(128)S(1)} %multiply_reduce_fusion, f32[6]{0:T(128)S(1)} %get-tuple-element.4), channel_id=1, replica_groups=mesh['dp'=64,'tensor'=4] {'tensor'}, use_global_device_ids=true, to_apply=%region_3.0 | all-reduce | flops 70 | bytes 560 | tf_op jit(solution)/shard_map/psum | solution.py:77
  129.5 247.4 %all-gather.6.cloned.1.call-done = bf16[64,6,2048]{2,1,0:T(8,128)(2,1)} async-done(((bf16[1,6,2048]{2,1,0:T(8,128)(2,1)}), bf16[64,6,2048]{2,1,0:T(8,128)(2,1)}) %all-gather.6.cloned.1.call-update) | async-done | bytes 1572880 | tf_op jit(solution)/shard_map/all_gather | solution.py:71
  376.9 2.6 reshape.32
  379.5 2.2 fusion.7
  381.7 0.0 all-reduce.3.cloned.1.call-update
  381.7 88.6 %all-reduce.3.cloned.1.call-done = f32[384,64]{0,1:T(8,128)} async-done(((f32[384,64]{0,1:T(8,128)}), f32[384,64]{0,1:T(8,128)}) %all-reduce.3.cloned.1.call-update) | async-done | bytes 98320 | tf_op jit(solution)/shard_map/psum | solution.py:77
  470.3 1.0 broadcast_multiply_fusion
  471.3 0.1 copy.23
  471.4 0.8 reshape.33
  472.2 10.2 %all-to-all-start = ((f32[64,1,384]{2,1,0:T(1,128)}), f32[64,1,384]{2,1,0:T(1,128)S(1)}, u32[]{:S(2)}, u32[]{:S(2)}) async-start(f32[64,1,384]{2,1,0:T(1,128)} %reshape.33), calls=%async_computation.1 | async-start | bytes 196608 | tf_op jit(solution)/shard_map/all_to_all | solution.py:79
  482.4 9.7 %all-to-all-done = f32[64,1,384]{2,1,0:T(1,128)S(1)} async-done(((f32[64,1,384]{2,1,0:T(1,128)}), f32[64,1,384]{2,1,0:T(1,128)S(1)}, u32[]{:S(2)}, u32[]{:S(2)}) %all-to-all-start) | async-done | bytes 98336 | tf_op jit(solution)/shard_map/all_to_all | solution.py:79
  492.1 0.5 broadcast.18
  492.7 0.9 reduce
  493.5 0.1 reshape.34
  493.7 0.1 all_to_all.17
  493.8 0.7 multiply_multiply_fusion
  (4 shorter events, 0.1 us)
Async XLA Ops:
  7.2 1.6 copy-start
  7.2 1.6 copy-start.2
  7.2 2.2 copy-start.4
  7.2 68.9 %all-gather.4.cloned.1.call-start = ((), (), s32[]{:S(2)}) async-start(), calls=%async_computation.2 | async-start | bytes 9830400 | tf_op jit(solution)/shard_map/all_gather | solution.py:47
  7.9 2.0 copy-start.3
  7.9 112.5 %reduce-scatter.2.cloned.1.call-start = ((), (), s32[]{:S(2)}) async-start(), calls=%async_computation.3 | async-start | bytes 327680 | tf_op jit(solution)/shard_map/reduce_scatter | solution.py:62
  9.4 66.7 %copy-start.5 = (bf16[128,128]{1,0:T(8,128)(2,1)S(1)}, bf16[128,128]{1,0:T(8,128)(2,1)}, u32[]{:S(2)}) copy-start(bf16[128,128]{1,0:T(8,128)(2,1)} %param.16) | copy-start | bytes 98308
  88.0 34.0 %copy-start.1 = (bf16[64,2048]{1,0:T(8,128)(2,1)S(1)}, bf16[64,2048]{1,0:T(8,128)(2,1)}, u32[]{:S(2)}) copy-start(bf16[64,2048]{1,0:T(8,128)(2,1)} %param.17) | copy-start | bytes 786436
  89.2 287.7 %all-gather.6.cloned.1.call-start = ((), (), s32[]{:S(2)}) async-start(), calls=%async_computation.5 | async-start | bytes 2129920 | tf_op jit(solution)/shard_map/all_gather | solution.py:71
  122.0 348.3 %all-reduce.3.cloned.1.call-start = ((), (), s32[]{:S(2)}) async-start(), calls=%async_computation.4 | async-start | bytes 196608 | tf_op jit(solution)/shard_map/psum | solution.py:77
  472.2 19.9 %all-to-all-start = ((f32[64,1,384]{2,1,0:T(1,128)}), f32[64,1,384]{2,1,0:T(1,128)S(1)}, u32[]{:S(2)}, u32[]{:S(2)}) async-start(f32[64,1,384]{2,1,0:T(1,128)} %reshape.33), calls=%async_computation.1 | async-start | bytes 196608 | tf_op jit(solution)/shard_map/all_to_all | solution.py:79
Sparse Core Ops, SparseCore 0:
  9.9 66.1 all-gather.3
  89.3 31.0 reduce-scatter.1
  122.9 253.9 all-gather.5
  381.9 88.4 all-reduce.2
where the time goes:
time: 501 us
  waiting for transfers between devices  443 us (88%)
  matrix products  16.2 us (3%)
  between operations  13.9 us (3%)
  starting transfers between devices  10.3 us (2%)
  blocking collectives  7.25 us (1%)
  local copies, waits for them, and re-layouts  5.19 us (1%)
  other arithmetic  5.04 us (1%)
    all_gather x1, waiting for transfers between devices, on_device(): lax.all_gather(train_grads, 'dp', axis=0, tiled=True)  247 us
    psum x1, waiting for transfers between devices, on_device(): lax.psum((columns, local_sq, train_sq), 'tensor')  88.6 us
    all_gather x1, waiting for transfers between devices, on_device(): lax.all_gather(output_gradient, 'tensor', axis=0, tiled=True)  65.5 us
    reduce_scatter x1, waiting for transfers between devices, on_device(): lax.psum_scatter(partial_grads, 'tensor', scatter_dimension=1, tiled=True)  31.2 us
    all_to_all x1, starting transfers between devices, on_device(): lax.all_to_all(scaled, 'dp', split_axis=0, concat_axis=1, tiled=True)  10.2 us
  transfers between devices with their start and end apart: 5, of which 5 were waited for; matrix products, arithmetic and copies ran while one was open for 0% of the time, Pallas kernels for 0%

commit v1 on v0

v1 whole, which is shorter than its diff:
```python
import math

import jax
import jax.numpy as jnp
from jax import lax
from jax.sharding import Mesh, PartitionSpec as P

SEQ = 128
PROJ = 8192
TENSOR = ("yh", "c")
GROUP = ("z", "yl")


def split_mesh(mesh):
    return Mesh(mesh.devices.reshape(8, 4, 2, 2, 2), ("z", "x", "yl", "yh", "c"))


def on_device(
    activations,
    output_gradient,
    shrinking_entries,
    expanding_entries,
    expanding_sketch,
    input_side_matrix,
    output_side_matrix,
    shrinking_sketch,
    heldout_gradient,
):
    f32, bf16 = jnp.float32, jnp.bfloat16
    count = activations.shape[0] // SEQ
    heldout = lax.all_gather(heldout_gradient, "x", axis=0, tiled=True)

    side_e = jnp.dot(output_gradient, output_side_matrix, preferred_element_type=f32).astype(bf16)
    back = lax.dot_general(
        output_gradient, expanding_entries, (((1,), (1,)), ((), ())), preferred_element_type=f32
    ).astype(bf16)
    side_f = jnp.dot(back, shrinking_sketch, preferred_element_type=f32).astype(bf16)

    low = jnp.dot(activations, shrinking_entries, preferred_element_type=f32)
    part_a = lax.dot_general(
        expanding_sketch, low, (((0,), (1,)), ((), ())),
        precision=lax.Precision.HIGHEST, preferred_element_type=f32,
    )
    part_c = lax.dot_general(
        input_side_matrix, activations, (((0,), (1,)), ((), ())), preferred_element_type=f32
    )
    parts = jnp.stack([part_a, part_c]).astype(bf16)
    parts = parts.reshape(4, 16, count, SEQ).transpose(0, 2, 1, 3).reshape(4, count * 16, SEQ)
    sides = jnp.stack([side_e, side_e, side_f, side_f])
    sent = jnp.concatenate([sides, parts], axis=1)
    got = lax.all_to_all(sent, TENSOR, 0, 0, tiled=True)

    rows = side_e.shape[0]
    right = got[:, :rows].reshape(count, SEQ, SEQ).astype(f32)
    left = jnp.sum(got[:, rows:].astype(f32), axis=0).reshape(count, 16, SEQ)
    grads = lax.dot_general(
        left, right, (((2,), (1,)), ((0,), (0,))), precision=lax.Precision.HIGHEST
    ) / SEQ
    grads = grads.astype(bf16)
    train_grads = grads.reshape(count, 16 * SEQ)

    peers = 16
    all_grads = lax.all_to_all(
        jnp.broadcast_to(grads.reshape(1, count * 16, SEQ), (peers, count * 16, SEQ)),
        GROUP, 0, 0, tiled=True,
    ).reshape(peers * count, 16 * SEQ)

    dots = lax.dot_general(
        all_grads, heldout, (((1,), (1,)), ((), ())), preferred_element_type=f32
    ).astype(bf16)
    held_f = heldout.astype(f32)
    val_part = jnp.sum(held_f * held_f, axis=1)
    grads_f = all_grads.astype(f32)
    train_part = jnp.sum(grads_f * grads_f, axis=1).reshape(peers, 1, count)
    high = train_part.astype(bf16)
    rest = (train_part - high.astype(f32)).astype(bf16)
    wide = dots.shape[1]
    train_row = jnp.concatenate(
        [high, rest, jnp.zeros((peers, 1, wide - 2 * count), bf16)], axis=2
    )
    val_row = jnp.broadcast_to(val_part.astype(bf16), (peers, 1, wide))
    block = jnp.concatenate([dots.reshape(peers, count, wide), val_row, train_row], axis=1)
    block = jnp.broadcast_to(block[:, None], (peers, 4, 8, wide)).reshape(peers * 4, 16, SEQ)
    placed = lax.all_to_all(block, GROUP + TENSOR, 0, 0, tiled=True)
    total = jnp.sum(placed.reshape(8, 2, 4, 8, wide).astype(f32), axis=2)
    train_sq = (total[0, 0, 7, :count] + total[0, 0, 7, count : 2 * count])[:, None]
    val_sq = total[:, :, 6:7]
    scores = total[:, :, :count] * lax.rsqrt(val_sq + 1e-06)
    scores = scores.reshape(8, 2, count, 4, wide // 4).transpose(2, 0, 3, 1, 4).reshape(count, -1)
    scores = scores * lax.rsqrt(train_sq + 1e-06) * math.sqrt(PROJ)
    return (scores, train_grads)


def solution(mesh):
    dp = ("z", "x", "yl")
    return jax.shard_map(
        on_device,
        mesh=split_mesh(mesh),
        in_specs=(
            P(dp, TENSOR),
            P(dp + TENSOR, None),
            P(TENSOR, None),
            P(),
            P(),
            P(TENSOR, None),
            P(),
            P(),
            P(dp, TENSOR),
        ),
        out_specs=(P(dp, None), P(dp, TENSOR)),
        check_vma=False,
    )
```

time: 501 us -> 91.9 us (0.18)
  waiting for transfers between devices: 443 us -> 33.6 us
  starting transfers between devices: 10.3 us -> 26 us
  blocking collectives: 7.25 us -> 0 us
  matrix products: 16.2 us -> 9.78 us
    all_gather x2 -> x1, waiting for transfers between devices: 313 us -> 0.23 us  [on_device(): heldout = lax.all_gather(heldout_gradient, 'x', axis=0, tiled=True)]
    psum x1 -> x0, waiting for transfers between devices: 88.6 us -> none  [on_device(): lax.psum((columns, local_sq, train_sq), 'tensor')]
    reduce_scatter x1 -> x0, waiting for transfers between devices: 31.2 us -> none  [on_device(): lax.psum_scatter(partial_grads, 'tensor', scatter_dimension=1, tiled=True)]
    all_to_all x1 -> x3, waiting for transfers between devices: 9.71 us -> 32.7 us  [the longest x1 13.5 us: on_device(): placed = lax.all_to_all(block, GROUP + TENSOR, 0, 0, tiled=True)]
    all_to_all x1 -> x3, starting transfers between devices: 10.2 us -> 26 us  [the longest x1 11.6 us: on_device(): placed = lax.all_to_all(block, GROUP + TENSOR, 0, 0, tiled=True)]
    psum x1 -> x0, blocking collectives: 7.25 us -> none  [on_device(): lax.psum((columns, local_sq, train_sq), 'tensor')]
    dot_general x8 -> x7, matrix products: 16.2 us -> 9.78 us  [the longest x1 2.73 us: on_device(): jnp.dot(back, shrinking_sketch, preferred_element_type=f32).astype(bf16)]
  transfers between devices with their start and end apart: 5 -> 4, of which waited for: 5 -> 4; matrix products, arithmetic and copies ran while one was open for 0% -> 3% of each run, Pallas kernels for 0% -> 0%
where the time goes in v1:
time: 91.9 us; the launch traced here: 91.5 us
  waiting for transfers between devices  33.6 us (37%)
  starting transfers between devices  26 us (28%)
  between operations  14.3 us (16%)
  matrix products  9.78 us (11%)
  local copies, waits for them, and re-layouts  5.34 us (6%)
  other arithmetic  2.52 us (3%)
    all_to_all x1, waiting for transfers between devices, on_device(): placed = lax.all_to_all(block, GROUP + TENSOR, 0, 0, tiled=True)  13.5 us
    all_to_all x1, waiting for transfers between devices, on_device(): lax.all_to_all(jnp.broadcast_to(grads.reshape(1, count * 16, SEQ), (peers...  12.9 us
    all_to_all x1, starting transfers between devices, on_device(): placed = lax.all_to_all(block, GROUP + TENSOR, 0, 0, tiled=True)  11.6 us
    all_to_all x1, starting transfers between devices, on_device(): lax.all_to_all(jnp.broadcast_to(grads.reshape(1, count * 16, SEQ), (peers...  7.71 us
    all_to_all x1, starting transfers between devices, on_device(): got = lax.all_to_all(sent, TENSOR, 0, 0, tiled=True)  6.65 us
    all_to_all x1, waiting for transfers between devices, on_device(): got = lax.all_to_all(sent, TENSOR, 0, 0, tiled=True)  6.31 us
    dot_general x1, matrix products, on_device(): jnp.dot(back, shrinking_sketch, preferred_element_type=f32).astype(bf16)  2.73 us
    dot_general x1, matrix products, on_device(): jnp.dot(output_gradient, output_side_matrix, preferred_element_type=f32)  2.21 us
  transfers between devices with their start and end apart: 4, of which 4 were waited for; matrix products, arithmetic and copies ran while one was open for 3% of the time, Pallas kernels for 0%

profile of v1, /device:TPU:1, one launch (start us, length us, event | category | flops | bytes accessed | tf_op | source)
XLA Modules:
  0.0 91.5 jit_solution(5432867732499797357)
XLA Ops:
  7.2 0.0 copy-start
  7.2 1.5 %copy-done = bf16[768,1280]{1,0:T(8,128)(2,1)S(1)} copy-done((bf16[768,1280]{1,0:T(8,128)(2,1)S(1)}, bf16[768,1280]{1,0:T(8,128)(2,1)}, u32[]{:S(2)}) %copy-start) | copy-done | bytes 1966104
  8.7 0.0 copy-start.3
  8.7 1.6 %fusion.2 = bf16[1,32,768]{2,1,0:T(8,128)(2,1)S(1)} fusion(bf16[1280,32]{0,1:T(8,128)(2,1)} %param.14, bf16[768,1280]{1,0:T(8,128)(2,1)S(1)} %copy-done), kind=kOutput, calls=%fused_computation.9 | convolution fusion | flops 62939136 | bytes 2097152 | tf_op jit(solution)/shard_map/dot_general | solution.py:44
  10.3 0.0 copy-done.3
  10.3 0.7 fusion.7
  11.0 0.0 copy-done.5
  11.1 0.5 fusion.3
  11.6 0.0 copy-start.4
  11.6 0.1 convert_element_type.80
  11.8 0.0 copy-done.2
  11.8 2.2 %fusion = bf16[1,192,128]{2,1,0:T(8,128)(2,1)S(1)} fusion(bf16[192,5120]{1,0:T(8,128)(2,1)} %param.10, bf16[5120,128]{1,0:T(8,128)(2,1)S(1)} %copy-done.2), kind=kOutput, calls=%fused_computation.7 | convolution fusion | flops 251682816 | bytes 3325952 | tf_op jit(solution)/shard_map/dot_general | solution.py:33
  14.0 0.0 copy-done.4
  14.0 2.7 %fusion.1 = bf16[1,192,128]{2,1,0:T(8,128)(2,1)S(1)} fusion(bf16[128,128]{1,0:T(8,128)(2,1)S(1)} %copy-done.4, bf16[192,5120]{1,0:T(8,128)(2,1)} %param.10, bf16[128,5120]{1,0:T(8,128)(2,1)} %param.12), kind=kOutput, calls=%fused_computation.8 | convolution fusion | flops 257998848 | bytes 3358720 | tf_op jit(solution)/shard_map/dot_general | solution.py:37
  16.7 0.8 pad_maximum_fusion
  17.5 6.7 %all-to-all-start = ((bf16[4,288,128]{2,1,0:T(8,128)(2,1)}), bf16[4,288,128]{2,1,0:T(8,128)(2,1)S(1)}, u32[]{:S(2)}, u32[]{:S(2)}) async-start(bf16[4,288,128]{2,1,0:T(8,128)(2,1)} %pad_maximum_fusion), calls=%async_computation | async-start | bytes 589824 | tf_op jit(solution)/shard_map/all_to_all | solution.py:51
  24.1 0.0 all-gather.2.cloned.1.call-start
  24.1 0.7 all-gather.2.cloned.1.call-update
  24.9 6.3 %all-to-all-done = bf16[4,288,128]{2,1,0:T(8,128)(2,1)S(1)} async-done(((bf16[4,288,128]{2,1,0:T(8,128)(2,1)}), bf16[4,288,128]{2,1,0:T(8,128)(2,1)S(1)}, u32[]{:S(2)}, u32[]{:S(2)}) %all-to-all-start) | async-done | bytes 294944 | tf_op jit(solution)/shard_map/all_to_all | solution.py:51
  31.2 0.3 fusion.4
  31.5 0.8 broadcast_in_dim.21
  32.3 7.7 %all-to-all-start.1 = ((bf16[16,96,128]{2,1,0:T(8,128)(2,1)}), bf16[16,96,128]{2,1,0:T(8,128)(2,1)S(1)}, u32[]{:S(2)}, u32[]{:S(2)}) async-start(bf16[16,96,128]{2,1,0:T(8,128)(2,1)} %broadcast_in_dim.21), calls=%async_computation.1 | async-start | bytes 786432 | tf_op jit(solution)/shard_map/all_to_all | solution.py:63
  40.0 0.1 pad.4.clone
  40.1 12.9 %all-to-all-done.1 = bf16[16,96,128]{2,1,0:T(8,128)(2,1)S(1)} async-done(((bf16[16,96,128]{2,1,0:T(8,128)(2,1)}), bf16[16,96,128]{2,1,0:T(8,128)(2,1)S(1)}, u32[]{:S(2)}, u32[]{:S(2)}) %all-to-all-start.1) | async-done | bytes 393248 | tf_op jit(solution)/shard_map/all_to_all | solution.py:63
  53.0 0.3 multiply_reduce_fusion.1
  53.3 0.1 reduce_sum.46
  53.4 0.1 reduce_sum.47
  53.5 0.1 reshape.102
  53.6 0.1 copy.30
  53.7 0.1 copy.33
  53.8 0.1 copy.32
  53.9 0.2 reshape.100
  54.1 0.2 all-gather.2.cloned.1.call-done
  54.3 1.8 %convolution_convert_fusion = bf16[96,256]{1,0:T(8,128)(2,1)S(1)} fusion(bf16[96,2048]{1,0:T(8,128)(2,1)S(1)} %reshape.100, bf16[256,2048]{1,0:T(8,128)(2,1)} %all-gather.2.cloned.1.call-done), kind=kOutput, calls=%fused_computation.1 | convolution fusion | flops 100687872 | bytes 1490944 | tf_op jit(solution)/shard_map/dot_general | solution.py:68
  56.1 0.0 copy-done.1
  56.1 0.3 multiply_reduce_fusion
  56.5 0.1 maximum_maximum_fusion
  56.6 0.8 reshape.103
  57.4 11.6 %all-to-all-start.2 = ((bf16[64,16,128]{2,1,0:T(8,128)(2,1)}), bf16[64,16,128]{2,1,0:T(8,128)(2,1)S(1)}, u32[]{:S(2)}, u32[]{:S(2)}) async-start(bf16[64,16,128]{2,1,0:T(8,128)(2,1)} %reshape.103), calls=%async_computation.2 | async-start | bytes 524288 | tf_op jit(solution)/shard_map/all_to_all | solution.py:84
  69.0 0.6 copy.40
  69.6 13.5 %all-to-all-done.2 = bf16[64,16,128]{2,1,0:T(8,128)(2,1)S(1)} async-done(((bf16[64,16,128]{2,1,0:T(8,128)(2,1)}), bf16[64,16,128]{2,1,0:T(8,128)(2,1)S(1)}, u32[]{:S(2)}, u32[]{:S(2)}) %all-to-all-start.2) | async-done | bytes 262176 | tf_op jit(solution)/shard_map/all_to_all | solution.py:84
  83.1 0.1 reshape.107
  83.2 0.1 rsqrt_bitcast_fusion
  83.3 0.1 copy.34
  83.4 0.1 reshape.104
  83.5 0.2 copy.35
  83.7 0.2 reshape.105
  83.9 0.7 multiply_multiply_fusion
  (16 shorter events, 0.2 us)
Async XLA Ops:
  7.2 1.6 %copy-start = (bf16[768,1280]{1,0:T(8,128)(2,1)S(1)}, bf16[768,1280]{1,0:T(8,128)(2,1)}, u32[]{:S(2)}) copy-start(bf16[768,1280]{1,0:T(8,128)(2,1)} %param.9) | copy-start | bytes 5898244
  8.7 1.6 %copy-start.3 = (bf16[1280,128]{1,0:T(8,128)(2,1)S(1)}, bf16[1280,128]{1,0:T(8,128)(2,1)}, u32[]{:S(2)}) copy-start(bf16[1280,128]{1,0:T(8,128)(2,1)} %param.11) | copy-start | bytes 983044
  8.7 2.3 %copy-start.5 = (f32[128,32]{0,1:T(8,128)S(1)}, f32[128,32]{0,1:T(8,128)}, u32[]{:S(2)}) copy-start(f32[128,32]{0,1:T(8,128)} %param.13) | copy-start | bytes 49156
  10.3 1.4 %copy-start.2 = (bf16[5120,128]{1,0:T(8,128)(2,1)S(1)}, bf16[5120,128]{1,0:T(8,128)(2,1)}, u32[]{:S(2)}) copy-start(bf16[5120,128]{1,0:T(8,128)(2,1)} %param.15) | copy-start | bytes 3932164
  11.6 2.4 %copy-start.4 = (bf16[128,128]{1,0:T(8,128)(2,1)S(1)}, bf16[128,128]{1,0:T(8,128)(2,1)}, u32[]{:S(2)}) copy-start(bf16[128,128]{1,0:T(8,128)(2,1)} %param.16) | copy-start | bytes 98308
  17.5 13.7 %all-to-all-start = ((bf16[4,288,128]{2,1,0:T(8,128)(2,1)}), bf16[4,288,128]{2,1,0:T(8,128)(2,1)S(1)}, u32[]{:S(2)}, u32[]{:S(2)}) async-start(bf16[4,288,128]{2,1,0:T(8,128)(2,1)} %pad_maximum_fusion), calls=%async_computation | async-start | bytes 589824 | tf_op jit(solution)/shard_map/all_to_all | solution.py:51
  24.1 30.2 %all-gather.2.cloned.1.call-start = ((), (), s32[]{:S(2)}) async-start(), calls=%async_computation.3 | async-start | bytes 1310720 | tf_op jit(solution)/shard_map/all_gather | solution.py:31
  32.3 20.7 %all-to-all-start.1 = ((bf16[16,96,128]{2,1,0:T(8,128)(2,1)}), bf16[16,96,128]{2,1,0:T(8,128)(2,1)S(1)}, u32[]{:S(2)}, u32[]{:S(2)}) async-start(bf16[16,96,128]{2,1,0:T(8,128)(2,1)} %broadcast_in_dim.21), calls=%async_computation.1 | async-start | bytes 786432 | tf_op jit(solution)/shard_map/all_to_all | solution.py:63
  54.3 1.8 %copy-start.1 = (bf16[256,2048]{1,0:T(8,128)(2,1)S(1)}, bf16[256,2048]{1,0:T(8,128)(2,1)}, u32[]{:S(2)}) copy-start(bf16[256,2048]{1,0:T(8,128)(2,1)} %all-gather.2.cloned.1.call-done) | copy-start | bytes 3145732
  57.4 25.7 %all-to-all-start.2 = ((bf16[64,16,128]{2,1,0:T(8,128)(2,1)}), bf16[64,16,128]{2,1,0:T(8,128)(2,1)S(1)}, u32[]{:S(2)}, u32[]{:S(2)}) async-start(bf16[64,16,128]{2,1,0:T(8,128)(2,1)} %reshape.103), calls=%async_computation.2 | async-start | bytes 524288 | tf_op jit(solution)/shard_map/all_to_all | solution.py:84
Sparse Core Ops, SparseCore 0:
  26.8 27.5 all-gather.1

commit v2 on v1

v2 whole, which is shorter than its diff:
```python
import functools
import math

import jax
import jax.numpy as jnp
from jax import lax
from jax.experimental import pallas as pl
from jax.experimental.pallas import tpu as pltpu
from jax.sharding import Mesh, PartitionSpec as P

SEQ = 128
PROJ = 8192
LANES = 128
TENSOR = ("yh", "c")
GROUP = ("z", "yl")
PEERS = 16
COUNT = 6
OWN = 192
HELD = 64
KROWS = 16
PART = COUNT * KROWS
f32, bf16 = jnp.float32, jnp.bfloat16
HIGHEST = lax.Precision.HIGHEST
VMEM = pl.BlockSpec(memory_space=pltpu.VMEM)
ANY = pl.BlockSpec(memory_space=pl.ANY)
NT = (((1,), (1,)), ((), ()))


def params():
    return pltpu.CompilerParams(vmem_limit_bytes=56 * 1024 * 1024)


def dot(a, b, precision=None):
    return jnp.dot(a, b, preferred_element_type=f32, precision=precision)


def dot_nt(a, b, precision=None):
    return lax.dot_general(a, b, NT, preferred_element_type=f32, precision=precision)


def factors(
    act_h, og_h, shr_h, exp_h, sketch_h, ism_h, osm_h, ss_h,
    send, keep,
    act, og, shr, exp, sketch, ism, osm, ss, sems,
):
    half_rows = act.shape[0] // 2
    depth = og.shape[1] // 4
    copies = {}

    def start(name, src, dst):
        copies[name] = pltpu.make_async_copy(src, dst, sems.at[len(copies)])
        copies[name].start()

    start("shr", shr_h, shr)
    start("ism", ism_h, ism)
    start("sketch", sketch_h, sketch)
    for i in range(2):
        rows = pl.ds(i * half_rows, half_rows)
        start(f"act{i}", act_h.at[rows], act.at[rows])
    for i in range(4):
        cols = pl.ds(i * depth, depth)
        start(f"og{i}", og_h.at[:, cols], og.at[:, cols])
        start(f"osm{i}", osm_h.at[cols], osm.at[cols])
        start(f"exp{i}", exp_h.at[:, cols], exp.at[:, cols])
    start("ss", ss_h, ss)

    yh = lax.axis_index("yh")
    for name in ("shr", "ism", "sketch"):
        copies[name].wait()
    for i in range(2):
        copies[f"act{i}"].wait()
        block = act[i * half_rows : (i + 1) * half_rows, :]
        low = dot(block, shr[...])
        part_a = dot_nt(sketch[...], low, HIGHEST).astype(bf16)
        part_c = dot_nt(ism[...], block).astype(bf16)
        for m in range(half_rows // SEQ):
            n = i * (half_rows // SEQ) + m
            toks = slice(m * SEQ, (m + 1) * SEQ)
            for h in range(2):
                row = OWN + h * PART + n * KROWS
                for here, mine, other in ((0, part_a, part_c), (1, part_c, part_a)):

                    @pl.when(yh == here)
                    def _(row=row, h=h, toks=toks, mine=mine, other=other):
                        ks = slice(h * KROWS, (h + 1) * KROWS)
                        keep[row : row + KROWS, :] = mine[ks, toks]
                        send[row : row + KROWS, :] = other[ks, toks]

    e = jnp.zeros((OWN, LANES), f32)
    back = jnp.zeros((OWN, LANES), f32)
    for i in range(4):
        cols = slice(i * depth, (i + 1) * depth)
        for name in ("og", "osm", "exp"):
            copies[f"{name}{i}"].wait()
        block = og[:, cols]
        e = e + dot(block, osm[cols, :])
        back = back + dot_nt(block, exp[:, cols])
    copies["ss"].wait()
    e = e.astype(bf16)
    f = dot(back.astype(bf16), ss[...]).astype(bf16)
    for here, mine, other in ((0, e, f), (1, f, e)):

        @pl.when(yh == here)
        def _(mine=mine, other=other):
            keep[:OWN, :] = mine
            send[:OWN, :] = other


def add_and_pack(keep, got, send, half):
    core = lax.axis_index("c")
    send[:OWN, :] = keep[:OWN, :]
    send[OWN : 2 * OWN, :] = got[:OWN, :]
    sums = [
        keep[OWN + h * PART : OWN + (h + 1) * PART, :].astype(f32)
        + got[OWN + h * PART : OWN + (h + 1) * PART, :].astype(f32)
        for h in range(2)
    ]
    for here in range(2):

        @pl.when(core == here)
        def _(here=here):
            half[...] = sums[here]
            send[2 * OWN :, :] = sums[1 - here].astype(bf16)


def products(keep, got, half, got2, copies, grads_out, right, flat):
    yh, core = lax.axis_index("yh"), lax.axis_index("c")

    def place(h, c, value):
        right[pl.ds(pl.multiple_of((h * 2 + c) * OWN, OWN), OWN), :] = value

    place(yh, core, keep[:OWN, :])
    place(1 - yh, core, got[:OWN, :])
    place(yh, 1 - core, got2[:OWN, :])
    place(1 - yh, 1 - core, got2[OWN : 2 * OWN, :])
    left = half[...] + got2[2 * OWN :, :].astype(f32)
    for n in range(COUNT):
        rows = slice(n * KROWS, (n + 1) * KROWS)
        prod = dot(left[rows], right[n * SEQ : (n + 1) * SEQ, :].astype(f32), HIGHEST)
        prod = (prod * (1.0 / SEQ)).astype(bf16)
        flat[rows, :] = prod.astype(f32)
        for p in range(PEERS):
            copies[p, rows, :] = prod
    for k in range(KROWS):
        grads_out[:, k * LANES : (k + 1) * LANES] = flat[
            pl.ds(k, COUNT, stride=KROWS), :
        ].astype(bf16)


def inner(got, held0, held1, held2, held3, out, flat, rows_of, held):
    x = lax.axis_index("x")
    for r, block in enumerate((held0, held1, held2, held3)):
        place = lax.rem(x + r, 4)
        held[pl.ds(pl.multiple_of(place * HELD, HELD), HELD), :] = block[...]
    for p in range(PEERS):
        flat[p * PART : (p + 1) * PART, :] = got[p].astype(f32)
    flat[PEERS * PART :, :] = jnp.zeros((2 * KROWS, LANES), f32)
    train_sq = jnp.zeros((PEERS * 8, LANES), f32)
    val_sq = jnp.zeros((4 * HELD, LANES), f32)
    for k in range(KROWS):
        lanes = slice(k * LANES, (k + 1) * LANES)
        g = jnp.concatenate(
            [flat[pl.ds(p * PART + k, 8, stride=KROWS), :] for p in range(PEERS)], axis=0
        )
        train_sq = train_sq + g * g
        rows_of[:, lanes] = g.astype(bf16)
        h = held[:, lanes].astype(f32)
        val_sq = val_sq + h * h
    ones = jnp.ones((8, LANES), f32)
    train_row = dot_nt(ones, train_sq, HIGHEST)
    val_row = dot_nt(ones, val_sq, HIGHEST)
    high = train_row.astype(bf16).astype(f32)
    norms = (high, train_row - high)
    dots = dot_nt(rows_of[...], held[...])
    row = lax.broadcasted_iota(jnp.int32, (8, LANES), 0)
    for p in range(PEERS):
        tiles = []
        for s in range(2):
            lanes = slice(s * LANES, (s + 1) * LANES)
            tile = dots[p * 8 : (p + 1) * 8, lanes]
            tile = jnp.where(row == 6, val_row[:, lanes], tile)
            tiles.append(jnp.where(row == 7, norms[s], tile))
        block = jnp.concatenate(tiles, axis=0).astype(bf16)
        for t in range(4):
            out[p * 4 + t] = block


def finish(got, out):
    place = lax.axis_index("z") * 2 + lax.axis_index("yl")

    def total(z, yl):
        first = (z * 2 + yl) * 4
        block = got[first].astype(f32)
        for t in range(1, 4):
            block = block + got[first + t].astype(f32)
        return block

    lane = lax.broadcasted_iota(jnp.int32, (8, LANES), 1)
    row = lax.broadcasted_iota(jnp.int32, (8, LANES), 0)
    train = None
    for z in range(8):
        pair = [total(z, yl) for yl in range(2)]
        if train is None:
            norm = pair[0][7:8, :] + pair[0][15:16, :]
            mine = jnp.where(lane == place * 8 + row, norm, 0.0)
            train = lax.rsqrt(jnp.sum(mine, axis=1, keepdims=True) + 1e-06) * math.sqrt(PROJ)
        for s in range(2):
            a, b = (
                block[s * 8 : (s + 1) * 8, :]
                * lax.rsqrt(block[s * 8 + 6 : s * 8 + 7, :] + 1e-06)
                * train
                for block in pair
            )
            even = jnp.where(lane < HELD, a, pltpu.roll(b, HELD, 1))
            odd = jnp.where(lane < HELD, pltpu.roll(a, HELD, 1), b)
            for q, tile in ((0, even), (1, odd)):
                at = (z * 4 + s * 2 + q) * LANES
                out[:, at : at + LANES] = tile[:COUNT]


def swap(value, axis):
    return lax.ppermute(value, axis, [(0, 1), (1, 0)])


def on_device(
    activations,
    output_gradient,
    shrinking_entries,
    expanding_entries,
    expanding_sketch,
    input_side_matrix,
    output_side_matrix,
    shrinking_sketch,
    heldout_gradient,
):
    shape = jax.ShapeDtypeStruct
    held = [heldout_gradient] + [
        lax.ppermute(heldout_gradient, "x", [((i + r) % 4, i) for i in range(4)])
        for r in (1, 2, 3)
    ]

    operands = (
        activations, output_gradient, shrinking_entries, expanding_entries,
        expanding_sketch.T, input_side_matrix.T, output_side_matrix, shrinking_sketch,
    )
    pack = shape((OWN + 2 * PART, LANES), bf16)
    send, keep = pl.pallas_call(
        factors,
        out_shape=(pack, pack),
        in_specs=[ANY] * 8,
        out_specs=(VMEM, VMEM),
        scratch_shapes=[pltpu.VMEM(v.shape, v.dtype) for v in operands]
        + [pltpu.SemaphoreType.DMA((18,))],
        compiler_params=params(),
        name="factors",
    )(*operands)
    got = swap(send, "yh")
    send2, half = pl.pallas_call(
        add_and_pack,
        out_shape=(shape((2 * OWN + PART, LANES), bf16), shape((PART, LANES), f32)),
        in_specs=[VMEM] * 2,
        out_specs=(VMEM, VMEM),
        compiler_params=params(),
        name="add_and_pack",
    )(keep, got)
    got2 = swap(send2, "c")
    copies, train_grads = pl.pallas_call(
        products,
        out_shape=(shape((PEERS, PART, LANES), bf16), shape((COUNT, KROWS * LANES), bf16)),
        in_specs=[VMEM] * 4,
        out_specs=(VMEM, VMEM),
        scratch_shapes=[
            pltpu.VMEM((COUNT * SEQ, LANES), bf16),
            pltpu.VMEM((PART, LANES), f32),
        ],
        compiler_params=params(),
        name="products",
    )(keep, got, half, got2)

    copies, *held = lax.optimization_barrier((copies, *held))
    all_grads = lax.all_to_all(copies, GROUP, 0, 0, tiled=True)
    blocks = pl.pallas_call(
        inner,
        out_shape=shape((PEERS * 4, 16, LANES), bf16),
        in_specs=[VMEM] * 5,
        out_specs=VMEM,
        scratch_shapes=[
            pltpu.VMEM((PEERS * PART + 2 * KROWS, LANES), f32),
            pltpu.VMEM((PEERS * 8, KROWS * LANES), bf16),
            pltpu.VMEM((4 * HELD, KROWS * LANES), bf16),
        ],
        compiler_params=params(),
        name="inner",
    )(all_grads, *held)
    placed = lax.all_to_all(blocks, GROUP + TENSOR, 0, 0, tiled=True)
    scores = pl.pallas_call(
        finish,
        out_shape=shape((COUNT, 4096), f32),
        in_specs=[VMEM],
        out_specs=VMEM,
        compiler_params=params(),
        name="finish",
    )(placed)
    return (scores, train_grads)


def solution(mesh):
    split = Mesh(mesh.devices.reshape(8, 4, 2, 2, 2), ("z", "x", "yl", "yh", "c"))
    dp = ("z", "x", "yl")
    return jax.shard_map(
        on_device,
        mesh=split,
        in_specs=(
            P(dp, TENSOR),
            P(dp + TENSOR, None),
            P(TENSOR, None),
            P(),
            P(),
            P(TENSOR, None),
            P(),
            P(),
            P(dp, TENSOR),
        ),
        out_specs=(P(dp, None), P(dp, TENSOR)),
        check_vma=False,
    )
```

time: 91.9 us -> 76.8 us (0.84)
  blocking collectives: 0 us -> 44.8 us
  waiting for transfers between devices: 33.6 us -> 3.45 us
  Pallas kernels: 0 us -> 15.4 us
  starting transfers between devices: 26 us -> 10.8 us
  between operations: 14.3 us -> 0.69 us
  matrix products: 9.78 us -> 0 us
  local copies, waits for them, and re-layouts: 5.34 us -> 1.3 us
  other arithmetic: 2.52 us -> 0 us
    all_to_all x0 -> x2, blocking collectives: none -> 44.8 us  [the longest x1 22.9 us: on_device(): all_grads = lax.all_to_all(copies, GROUP, 0, 0, tiled=True)]
    all_to_all x3 -> x0, waiting for transfers between devices: 32.7 us -> none  [the longest x1 13.5 us: on_device(): placed = lax.all_to_all(block, GROUP + TENSOR, 0, 0, tiled=True)]
    all_to_all x3 -> x0, starting transfers between devices: 26 us -> none  [the longest x1 11.6 us: on_device(): placed = lax.all_to_all(block, GROUP + TENSOR, 0, 0, tiled=True)]
    pallas_call x0 -> x5, Pallas kernels: none -> 15.4 us  [the longest x1 6.53 us: on_device(): pl.pallas_call(factors, out_shape=(pack, pack), in_specs=[ANY] * 8, out_s...]
    ppermute x0 -> x5, starting transfers between devices: none -> 10.8 us  [the longest x2 5.68 us: swap(): return lax.ppermute(value, axis, [(0, 1), (1, 0)])]
    dot_general x7 -> x0, matrix products: 9.78 us -> none  [the longest x1 2.73 us: on_device(): jnp.dot(back, shrinking_sketch, preferred_element_type=f32).astype(bf16)]
    ppermute x0 -> x5, waiting for transfers between devices: none -> 3.45 us  [the longest x2 3.45 us: swap(): return lax.ppermute(value, axis, [(0, 1), (1, 0)])]
    reshape x7 -> x0, local copies, waits for them, and re-layouts: 1.48 us -> none  [the longest x1 0.78 us: on_device(): jnp.broadcast_to(block[:, None], (peers, 4, 8, wide))]
  transfers between devices with their start and end apart: 4 -> 5, of which waited for: 4 -> 2; matrix products, arithmetic and copies ran while one was open for 3% -> 0% of each run, Pallas kernels for 0% -> 14%
where the time goes in v2:
time: 76.8 us; the launch traced here: 76.5 us
  blocking collectives  44.8 us (58%)
  Pallas kernels  15.4 us (20%)
  starting transfers between devices  10.8 us (14%)
  waiting for transfers between devices  3.45 us (4%)
  local copies, waits for them, and re-layouts  1.3 us (2%)
    all_to_all x1, blocking collectives, on_device(): all_grads = lax.all_to_all(copies, GROUP, 0, 0, tiled=True)  22.9 us
    all_to_all x1, blocking collectives, on_device(): placed = lax.all_to_all(blocks, GROUP + TENSOR, 0, 0, tiled=True)  21.9 us
    pallas_call x1, Pallas kernels, on_device(): pl.pallas_call(factors, out_shape=(pack, pack), in_specs=[ANY] * 8, out_s...  6.53 us
    ppermute x2, starting transfers between devices, swap(): return lax.ppermute(value, axis, [(0, 1), (1, 0)])  5.68 us
    ppermute x3, starting transfers between devices, on_device(): lax.ppermute(heldout_gradient, 'x', [((i + r) % 4, i) for i in range(4)])  5.13 us
    ppermute x2, waiting for transfers between devices, swap(): return lax.ppermute(value, axis, [(0, 1), (1, 0)])  3.45 us
    pallas_call x1, Pallas kernels, on_device(): pl.pallas_call(inner, out_shape=shape((PEERS * 4, 16, LANES), bf16), in_s...  3.27 us
    pallas_call x1, Pallas kernels, on_device(): pl.pallas_call(products, out_shape=(shape((PEERS, PART, LANES), bf16), sh...  2.22 us
  transfers between devices with their start and end apart: 5, of which 2 were waited for; matrix products, arithmetic and copies ran while one was open for 0% of the time, Pallas kernels for 14%

profile of v2, /device:TPU:1, one launch (start us, length us, event | category | flops | bytes accessed | tf_op | source)
XLA Modules:
  0.0 76.5 jit_solution(6491781158702845047)
XLA Ops:
  0.6 3.7 %collective-permute-start.3 = (bf16[64,2048]{1,0:T(8,128)(2,1)}, bf16[64,2048]{1,0:T(8,128)(2,1)S(1)}, u32[]{:S(2)}, u32[]{:S(2)}) collective-permute-start(bf16[64,2048]{1,0:T(8,128)(2,1)} %held0), channel_id=1, source_target_pairs={{16,0},{24,8},{0,16},{8,24},{17,1},{25,9},{1,17},{9,25},{18,2},{26... | collective-permute-start | bytes 786440 | tf_op jit(solution)/shard_map/ppermute | solution.py:238
  4.3 0.9 %collective-permute-start.2 = (bf16[64,2048]{1,0:T(8,128)(2,1)}, bf16[64,2048]{1,0:T(8,128)(2,1)S(1)}, u32[]{:S(2)}, u32[]{:S(2)}) collective-permute-start(bf16[64,2048]{1,0:T(8,128)(2,1)} %held0), channel_id=1, source_target_pairs={{8,0},{16,8},{24,16},{0,24},{9,1},{17,9},{25,17},{1,25},{10,2},{18... | collective-permute-start | bytes 786440 | tf_op jit(solution)/shard_map/ppermute | solution.py:238
  5.2 0.6 collective-permute-start.4
  5.8 6.5 %factors.1 = (bf16[384,128]{1,0:T(8,128)(2,1)}, bf16[384,128]{1,0:T(8,128)(2,1)}) custom-call(bf16[768,1280]{1,0:T(8,128)(2,1)} %act_h.1, bf16[192,5120]{1,0:T(8,128)(2,1)} %og_h.1, bf16[1280,128]{1,0:T(8,128)(2,1)} %shr_h.1, bf16[128,5120]{1,0:T(8,128)(2,1)} %exp_h.1, f32[32,128]{1,0:T(8,128)} %bitcast.3, bf16[32,1280]{1,0:T(8,128)(2,1)} %bitcast.2, ...), custom_call_target="tpu_custom_call" | custom-call | tf_op jit(solution)/shard_map/factors/pallas_call | solution.py:247
  12.3 3.0 %collective-permute-start = (bf16[384,128]{1,0:T(8,128)(2,1)}, bf16[384,128]{1,0:T(8,128)(2,1)S(1)}, u32[]{:S(2)}, u32[]{:S(2)}) collective-permute-start(bf16[384,128]{1,0:T(8,128)(2,1)} %get-tuple-element.14), channel_id=1, source_target_pairs={{0,2},{2,0},{1,3},{3,1},{4,6},{6,4},{5,7},{7,5},{8,10},{10,8},{9,1... | collective-permute-start | bytes 294920 | tf_op jit(solution)/shard_map/ppermute | solution.py:222
  15.3 2.3 %collective-permute-done.got = bf16[384,128]{1,0:T(8,128)(2,1)S(1)} collective-permute-done((bf16[384,128]{1,0:T(8,128)(2,1)}, bf16[384,128]{1,0:T(8,128)(2,1)S(1)}, u32[]{:S(2)}, u32[]{:S(2)}) %collective-permute-start) | collective-permute-done | bytes 98336 | tf_op jit(solution)/shard_map/ppermute | solution.py:222
  17.6 0.0 copy-start
  17.6 0.6 copy-done
  18.2 1.6 %add_and_pack.1 = (bf16[480,128]{1,0:T(8,128)(2,1)}, f32[96,128]{1,0:T(8,128)}) custom-call(bf16[384,128]{1,0:T(8,128)(2,1)} %get-tuple-element.13.keep, bf16[384,128]{1,0:T(8,128)(2,1)} %copy-done), custom_call_target="tpu_custom_call" | custom-call | tf_op jit(solution)/shard_map/add_and_pack/pallas_call | solution.py:258
  19.8 2.7 %collective-permute-start.1 = (bf16[480,128]{1,0:T(8,128)(2,1)}, bf16[480,128]{1,0:T(8,128)(2,1)S(1)}, u32[]{:S(2)}, u32[]{:S(2)}) collective-permute-start(bf16[480,128]{1,0:T(8,128)(2,1)} %get-tuple-element.16), channel_id=1, source_target_pairs={{0,1},{1,0},{2,3},{3,2},{4,5},{5,4},{6,7},{7,6},{8,9},{9,8},{10,11... | collective-permute-start | bytes 368648 | tf_op jit(solution)/shard_map/ppermute | solution.py:222
  22.5 1.2 %collective-permute-done.1.got2 = bf16[480,128]{1,0:T(8,128)(2,1)S(1)} collective-permute-done((bf16[480,128]{1,0:T(8,128)(2,1)}, bf16[480,128]{1,0:T(8,128)(2,1)S(1)}, u32[]{:S(2)}, u32[]{:S(2)}) %collective-permute-start.1) | collective-permute-done | bytes 122912 | tf_op jit(solution)/shard_map/ppermute | solution.py:222
  23.7 0.0 copy-start.4
  23.7 0.6 copy-done.4
  24.3 2.2 %products.1 = (bf16[16,96,128]{2,1,0:T(8,128)(2,1)}, bf16[6,2048]{1,0:T(8,128)(2,1)}) custom-call(bf16[384,128]{1,0:T(8,128)(2,1)} %get-tuple-element.13.keep, bf16[384,128]{1,0:T(8,128)(2,1)} %copy-done, f32[96,128]{1,0:T(8,128)} %get-tuple-element.15.half, bf16[480,128]{1,0:T(8,128)(2,1)} %copy-done.4), custom_call_target="tpu_custom_call" | custom-call | tf_op jit(solution)/shard_map/products/pallas_call | solution.py:267
  26.5 0.0 collective-permute-done.3.held2
  26.5 0.0 copy-start.1
  26.5 0.0 collective-permute-done.2.held1
  26.6 0.0 copy-start.2
  26.6 0.0 collective-permute-done.4.held3
  26.6 0.0 copy-start.3
  26.6 22.9 %all_to_all.10.got = bf16[16,96,128]{2,1,0:T(8,128)(2,1)} all-to-all(bf16[16,96,128]{2,1,0:T(8,128)(2,1)} %get-tuple-element.18), channel_id=1, replica_groups=mesh['z'=8,'x'=4,'yl'=2,'yh'=2,'c'=2] {'z','yl'}, dimensions={0} | all-to-all | bytes 786432 | tf_op jit(solution)/shard_map/all_to_all | solution.py:281
  49.5 0.0 copy-done.1
  49.5 0.0 copy-done.2
  49.5 0.0 copy-done.3
  49.5 3.3 %inner.1 = bf16[64,16,128]{2,1,0:T(8,128)(2,1)} custom-call(bf16[16,96,128]{2,1,0:T(8,128)(2,1)} %all_to_all.10.got, bf16[64,2048]{1,0:T(8,128)(2,1)} %held0, bf16[64,2048]{1,0:T(8,128)(2,1)} %copy-done.2, bf16[64,2048]{1,0:T(8,128)(2,1)} %copy-done.1, bf16[64,2048]{1,0:T(8,128)(2,1)} %copy-done.3), custom_call_target="tpu_custom_call" | custom-call | tf_op jit(solution)/shard_map/inner/pallas_call | solution.py:282
  52.8 21.9 %all_to_all.11.got = bf16[64,16,128]{2,1,0:T(8,128)(2,1)} all-to-all(bf16[64,16,128]{2,1,0:T(8,128)(2,1)} %inner.1), channel_id=1, replica_groups=mesh['z'=8,'x'=4,'yl'=2,'yh'=2,'c'=2] {'z','yl','yh','c'}, dimensions={0} | all-to-all | bytes 524288 | tf_op jit(solution)/shard_map/all_to_all | solution.py:295
  74.7 1.8 %finish.1 = f32[6,4096]{1,0:T(8,128)} custom-call(bf16[64,16,128]{2,1,0:T(8,128)(2,1)} %all_to_all.11.got), custom_call_target="tpu_custom_call" | custom-call | tf_op jit(solution)/shard_map/finish/pallas_call | solution.py:296
Async XLA Ops:
  0.6 25.9 %collective-permute-start.3 = (bf16[64,2048]{1,0:T(8,128)(2,1)}, bf16[64,2048]{1,0:T(8,128)(2,1)S(1)}, u32[]{:S(2)}, u32[]{:S(2)}) collective-permute-start(bf16[64,2048]{1,0:T(8,128)(2,1)} %held0), channel_id=1, source_target_pairs={{16,0},{24,8},{0,16},{8,24},{17,1},{25,9},{1,17},{9,25},{18,2},{26... | collective-permute-start | bytes 786440 | tf_op jit(solution)/shard_map/ppermute | solution.py:238
  4.3 22.3 %collective-permute-start.2 = (bf16[64,2048]{1,0:T(8,128)(2,1)}, bf16[64,2048]{1,0:T(8,128)(2,1)S(1)}, u32[]{:S(2)}, u32[]{:S(2)}) collective-permute-start(bf16[64,2048]{1,0:T(8,128)(2,1)} %held0), channel_id=1, source_target_pairs={{8,0},{16,8},{24,16},{0,24},{9,1},{17,9},{25,17},{1,25},{10,2},{18... | collective-permute-start | bytes 786440 | tf_op jit(solution)/shard_map/ppermute | solution.py:238
  5.2 21.4 %collective-permute-start.4 = (bf16[64,2048]{1,0:T(8,128)(2,1)}, bf16[64,2048]{1,0:T(8,128)(2,1)S(1)}, u32[]{:S(2)}, u32[]{:S(2)}) collective-permute-start(bf16[64,2048]{1,0:T(8,128)(2,1)} %held0), channel_id=1, source_target_pairs={{24,0},{0,8},{8,16},{16,24},{25,1},{1,9},{9,17},{17,25},{26,2},{2,... | collective-permute-start | bytes 786440 | tf_op jit(solution)/shard_map/ppermute | solution.py:238
  12.3 5.3 %collective-permute-start = (bf16[384,128]{1,0:T(8,128)(2,1)}, bf16[384,128]{1,0:T(8,128)(2,1)S(1)}, u32[]{:S(2)}, u32[]{:S(2)}) collective-permute-start(bf16[384,128]{1,0:T(8,128)(2,1)} %get-tuple-element.14), channel_id=1, source_target_pairs={{0,2},{2,0},{1,3},{3,1},{4,6},{6,4},{5,7},{7,5},{8,10},{10,8},{9,1... | collective-permute-start | bytes 294920 | tf_op jit(solution)/shard_map/ppermute | solution.py:222
  17.6 0.6 copy-start
  19.8 3.9 %collective-permute-start.1 = (bf16[480,128]{1,0:T(8,128)(2,1)}, bf16[480,128]{1,0:T(8,128)(2,1)S(1)}, u32[]{:S(2)}, u32[]{:S(2)}) collective-permute-start(bf16[480,128]{1,0:T(8,128)(2,1)} %get-tuple-element.16), channel_id=1, source_target_pairs={{0,1},{1,0},{2,3},{3,2},{4,5},{5,4},{6,7},{7,6},{8,9},{9,8},{10,11... | collective-permute-start | bytes 368648 | tf_op jit(solution)/shard_map/ppermute | solution.py:222
  23.7 0.6 copy-start.4
  26.5 23.0 %copy-start.1 = (bf16[64,2048]{1,0:T(8,128)(2,1)}, bf16[64,2048]{1,0:T(8,128)(2,1)S(1)}, u32[]{:S(2)}) copy-start(bf16[64,2048]{1,0:T(8,128)(2,1)S(1)} %collective-permute-done.3.held2) | copy-start | bytes 786436
  26.6 22.9 %copy-start.2 = (bf16[64,2048]{1,0:T(8,128)(2,1)}, bf16[64,2048]{1,0:T(8,128)(2,1)S(1)}, u32[]{:S(2)}) copy-start(bf16[64,2048]{1,0:T(8,128)(2,1)S(1)} %collective-permute-done.2.held1) | copy-start | bytes 786436
  26.6 22.9 %copy-start.3 = (bf16[64,2048]{1,0:T(8,128)(2,1)}, bf16[64,2048]{1,0:T(8,128)(2,1)S(1)}, u32[]{:S(2)}) copy-start(bf16[64,2048]{1,0:T(8,128)(2,1)S(1)} %collective-permute-done.4.held3) | copy-start | bytes 786436

commit v3 on v2

--- a/solution.py
+++ b/solution.py
@@ -22,12 +22,12 @@
 f32, bf16 = jnp.float32, jnp.bfloat16
 HIGHEST = lax.Precision.HIGHEST
 VMEM = pl.BlockSpec(memory_space=pltpu.VMEM)
-ANY = pl.BlockSpec(memory_space=pl.ANY)
+HBM = pl.BlockSpec(memory_space=pltpu.HBM)
 NT = (((1,), (1,)), ((), ()))
 
 
-def params():
-    return pltpu.CompilerParams(vmem_limit_bytes=56 * 1024 * 1024)
+def params(mib):
+    return pltpu.CompilerParams(vmem_limit_bytes=mib * 1024 * 1024)
 
 
 def dot(a, b, precision=None):
@@ -247,20 +247,20 @@
     send, keep = pl.pallas_call(
         factors,
         out_shape=(pack, pack),
-        in_specs=[ANY] * 8,
+        in_specs=[HBM] * 8,
         out_specs=(VMEM, VMEM),
         scratch_shapes=[pltpu.VMEM(v.shape, v.dtype) for v in operands]
         + [pltpu.SemaphoreType.DMA((18,))],
-        compiler_params=params(),
+        compiler_params=params(16),
         name="factors",
-    )(*operands)
+    )(*(pltpu.with_memory_space_constraint(v, pltpu.HBM) for v in operands))
     got = swap(send, "yh")
     send2, half = pl.pallas_call(
         add_and_pack,
         out_shape=(shape((2 * OWN + PART, LANES), bf16), shape((PART, LANES), f32)),
         in_specs=[VMEM] * 2,
         out_specs=(VMEM, VMEM),
-        compiler_params=params(),
+        compiler_params=params(4),
         name="add_and_pack",
     )(keep, got)
     got2 = swap(send2, "c")
@@ -273,7 +273,7 @@
             pltpu.VMEM((COUNT * SEQ, LANES), bf16),
             pltpu.VMEM((PART, LANES), f32),
         ],
-        compiler_params=params(),
+        compiler_params=params(4),
         name="products",
     )(keep, got, half, got2)
 
@@ -289,7 +289,7 @@
             pltpu.VMEM((PEERS * 8, KROWS * LANES), bf16),
             pltpu.VMEM((4 * HELD, KROWS * LANES), bf16),
         ],
-        compiler_params=params(),
+        compiler_params=params(12),
         name="inner",
     )(all_grads, *held)
     placed = lax.all_to_all(blocks, GROUP + TENSOR, 0, 0, tiled=True)
@@ -298,7 +298,7 @@
         out_shape=shape((COUNT, 4096), f32),
         in_specs=[VMEM],
         out_specs=VMEM,
-        compiler_params=params(),
+        compiler_params=params(4),
         name="finish",
     )(placed)
     return (scores, train_grads)

time: 76.8 us -> 68 us (0.89)
  Pallas kernels: 15.4 us -> 9.1 us
  local copies, waits for them, and re-layouts: 1.3 us -> 0.01 us
    pallas_call x1, Pallas kernels: 3.27 us -> 1.25 us  [on_device(): pl.pallas_call(inner, out_shape=shape((PEERS * 4, 16, LANES), bf16), in_s...]
    pallas_call x1, Pallas kernels: 1.61 us -> 0.02 us  [on_device(): pl.pallas_call(add_and_pack, out_shape=(shape((2 * OWN + PART, LANES), bf...]
    unnamed x10 -> x2, local copies, waits for them, and re-layouts: 1.3 us -> 0.01 us
    pallas_call x1, Pallas kernels: 2.22 us -> 1.09 us  [on_device(): pl.pallas_call(products, out_shape=(shape((PEERS, PART, LANES), bf16), sh...]
    pallas_call x1, Pallas kernels: 1.81 us -> 0.86 us  [on_device(): pl.pallas_call(finish, out_shape=shape((COUNT, 4096), f32), in_specs=[VME...]
  transfers between devices with their start and end apart: 5 -> 5, of which waited for: 2 -> 2; matrix products, arithmetic and copies ran while one was open for 0% -> 0% of each run, Pallas kernels for 14% -> 10%
where the time goes in v3:
time: 68 us; the launch traced here: 67.9 us
  blocking collectives  44.2 us (65%)
  starting transfers between devices  10.9 us (16%)
  Pallas kernels  9.1 us (13%)
  waiting for transfers between devices  3.03 us (4%)
    all_to_all x1, blocking collectives, on_device(): all_grads = lax.all_to_all(copies, GROUP, 0, 0, tiled=True)  22.6 us
    all_to_all x1, blocking collectives, on_device(): placed = lax.all_to_all(blocks, GROUP + TENSOR, 0, 0, tiled=True)  21.6 us
    pallas_call x1, Pallas kernels, on_device(): pl.pallas_call(factors, out_shape=(pack, pack), in_specs=[HBM] * 8, out_s...  5.89 us
    ppermute x2, starting transfers between devices, swap(): return lax.ppermute(value, axis, [(0, 1), (1, 0)])  5.77 us
    ppermute x3, starting transfers between devices, on_device(): lax.ppermute(heldout_gradient, 'x', [((i + r) % 4, i) for i in range(4)])  5.13 us
    ppermute x2, waiting for transfers between devices, swap(): return lax.ppermute(value, axis, [(0, 1), (1, 0)])  3.02 us
  transfers between devices with their start and end apart: 5, of which 2 were waited for; matrix products, arithmetic and copies ran while one was open for 0% of the time, Pallas kernels for 10%

profile of v3, /device:TPU:1, one launch (start us, length us, event | category | flops | bytes accessed | tf_op | source)
XLA Modules:
  0.0 67.9 jit_solution(11462707038045294315)
XLA Ops:
  0.6 3.7 %collective-permute-start.3 = (bf16[64,2048]{1,0:T(8,128)(2,1)}, bf16[64,2048]{1,0:T(8,128)(2,1)S(1)}, u32[]{:S(2)}, u32[]{:S(2)}) collective-permute-start(bf16[64,2048]{1,0:T(8,128)(2,1)} %held0), channel_id=1, source_target_pairs={{16,0},{24,8},{0,16},{8,24},{17,1},{25,9},{1,17},{9,25},{18,2},{26... | collective-permute-start | bytes 786440 | tf_op jit(solution)/shard_map/ppermute | solution.py:238
  4.3 0.9 %collective-permute-start.2 = (bf16[64,2048]{1,0:T(8,128)(2,1)}, bf16[64,2048]{1,0:T(8,128)(2,1)S(1)}, u32[]{:S(2)}, u32[]{:S(2)}) collective-permute-start(bf16[64,2048]{1,0:T(8,128)(2,1)} %held0), channel_id=1, source_target_pairs={{8,0},{16,8},{24,16},{0,24},{9,1},{17,9},{25,17},{1,25},{10,2},{18... | collective-permute-start | bytes 786440 | tf_op jit(solution)/shard_map/ppermute | solution.py:238
  5.2 0.6 collective-permute-start.4
  5.8 0.0 copy-start
  5.8 5.9 %factors.1 = (bf16[384,128]{1,0:T(8,128)(2,1)S(1)}, bf16[384,128]{1,0:T(8,128)(2,1)S(1)}) custom-call(bf16[768,1280]{1,0:T(8,128)(2,1)} %act_h.1, bf16[192,5120]{1,0:T(8,128)(2,1)} %og_h.1, bf16[1280,128]{1,0:T(8,128)(2,1)} %shr_h.1, bf16[128,5120]{1,0:T(8,128)(2,1)} %exp_h.1, f32[32,128]{1,0:T(8,128)} %bitcast.3, bf16[32,1280]{1,0:T(8,128)(2,1)} %bitcast.2, ...), custom_call_target="tpu_custom_call" | custom-call | tf_op jit(solution)/shard_map/factors/pallas_call | solution.py:247
  11.7 3.0 %collective-permute-start = (bf16[384,128]{1,0:T(8,128)(2,1)S(1)}, bf16[384,128]{1,0:T(8,128)(2,1)S(1)}, u32[]{:S(2)}, u32[]{:S(2)}) collective-permute-start(bf16[384,128]{1,0:T(8,128)(2,1)S(1)} %get-tuple-element.14), channel_id=1, source_target_pairs={{0,2},{2,0},{1,3},{3,1},{4,6},{6,4},{5,7},{7,5},{8,10},{10,8},{9,1... | collective-permute-start | bytes 294920 | tf_op jit(solution)/shard_map/ppermute | solution.py:222
  14.7 2.0 %collective-permute-done.got = bf16[384,128]{1,0:T(8,128)(2,1)S(1)} collective-permute-done((bf16[384,128]{1,0:T(8,128)(2,1)S(1)}, bf16[384,128]{1,0:T(8,128)(2,1)S(1)}, u32[]{:S(2)}, u32[]{:S(2)}) %collective-permute-start) | collective-permute-done | bytes 98336 | tf_op jit(solution)/shard_map/ppermute | solution.py:222
  16.7 2.8 %collective-permute-start.1 = (bf16[480,128]{1,0:T(8,128)(2,1)S(1)}, bf16[480,128]{1,0:T(8,128)(2,1)S(1)}, u32[]{:S(2)}, u32[]{:S(2)}) collective-permute-start(bf16[480,128]{1,0:T(8,128)(2,1)S(1)} %get-tuple-element.16), channel_id=1, source_target_pairs={{0,1},{1,0},{2,3},{3,2},{4,5},{5,4},{6,7},{7,6},{8,9},{9,8},{10,11... | collective-permute-start | bytes 368648 | tf_op jit(solution)/shard_map/ppermute | solution.py:222
  19.5 1.0 %collective-permute-done.1.got2 = bf16[480,128]{1,0:T(8,128)(2,1)S(1)} collective-permute-done((bf16[480,128]{1,0:T(8,128)(2,1)S(1)}, bf16[480,128]{1,0:T(8,128)(2,1)S(1)}, u32[]{:S(2)}, u32[]{:S(2)}) %collective-permute-start.1) | collective-permute-done | bytes 122912 | tf_op jit(solution)/shard_map/ppermute | solution.py:222
  20.5 1.1 %products.1 = (bf16[16,96,128]{2,1,0:T(8,128)(2,1)S(1)}, bf16[6,2048]{1,0:T(8,128)(2,1)}) custom-call(bf16[384,128]{1,0:T(8,128)(2,1)S(1)} %get-tuple-element.13.keep, bf16[384,128]{1,0:T(8,128)(2,1)S(1)} %collective-permute-done.got, f32[96,128]{1,0:T(8,128)S(1)} %get-tuple-element.15.half, bf16[480,128]{1,0:T(8,128)(2,1)S(1)} %collective-permute-done.1.got2), custom_call_target="tpu_custom_call" | custom-call | tf_op jit(solution)/shard_map/products/pallas_call | solution.py:267
  21.6 0.0 collective-permute-done.3.held2
  21.6 0.0 collective-permute-done.2.held1
  21.6 0.0 collective-permute-done.4.held3
  21.6 22.6 %all_to_all.10.got = bf16[16,96,128]{2,1,0:T(8,128)(2,1)S(1)} all-to-all(bf16[16,96,128]{2,1,0:T(8,128)(2,1)S(1)} %get-tuple-element.18), channel_id=1, replica_groups=mesh['z'=8,'x'=4,'yl'=2,'yh'=2,'c'=2] {'z','yl'}, dimensions={0} | all-to-all | bytes 786432 | tf_op jit(solution)/shard_map/all_to_all | solution.py:281
  44.2 0.0 copy-done
  44.2 1.3 %inner.1 = bf16[64,16,128]{2,1,0:T(8,128)(2,1)S(1)} custom-call(bf16[16,96,128]{2,1,0:T(8,128)(2,1)S(1)} %all_to_all.10.got, bf16[64,2048]{1,0:T(8,128)(2,1)S(1)} %copy-done, bf16[64,2048]{1,0:T(8,128)(2,1)S(1)} %collective-permute-done.2.held1, bf16[64,2048]{1,0:T(8,128)(2,1)S(1)} %collective-permute-done.3.held2, ...), custom_call_target="tpu_custom_call" | custom-call | tf_op jit(solution)/shard_map/inner/pallas_call | solution.py:282
  45.4 21.6 %all_to_all.11.got = bf16[64,16,128]{2,1,0:T(8,128)(2,1)S(1)} all-to-all(bf16[64,16,128]{2,1,0:T(8,128)(2,1)S(1)} %inner.1), channel_id=1, replica_groups=mesh['z'=8,'x'=4,'yl'=2,'yh'=2,'c'=2] {'z','yl','yh','c'}, dimensions={0} | all-to-all | bytes 524288 | tf_op jit(solution)/shard_map/all_to_all | solution.py:295
  67.0 0.9 %finish.1 = f32[6,4096]{1,0:T(8,128)} custom-call(bf16[64,16,128]{2,1,0:T(8,128)(2,1)S(1)} %all_to_all.11.got), custom_call_target="tpu_custom_call" | custom-call | tf_op jit(solution)/shard_map/finish/pallas_call | solution.py:296
  (1 shorter events, 0.0 us)
Async XLA Ops:
  0.6 20.9 %collective-permute-start.3 = (bf16[64,2048]{1,0:T(8,128)(2,1)}, bf16[64,2048]{1,0:T(8,128)(2,1)S(1)}, u32[]{:S(2)}, u32[]{:S(2)}) collective-permute-start(bf16[64,2048]{1,0:T(8,128)(2,1)} %held0), channel_id=1, source_target_pairs={{16,0},{24,8},{0,16},{8,24},{17,1},{25,9},{1,17},{9,25},{18,2},{26... | collective-permute-start | bytes 786440 | tf_op jit(solution)/shard_map/ppermute | solution.py:238
  4.3 17.3 %collective-permute-start.2 = (bf16[64,2048]{1,0:T(8,128)(2,1)}, bf16[64,2048]{1,0:T(8,128)(2,1)S(1)}, u32[]{:S(2)}, u32[]{:S(2)}) collective-permute-start(bf16[64,2048]{1,0:T(8,128)(2,1)} %held0), channel_id=1, source_target_pairs={{8,0},{16,8},{24,16},{0,24},{9,1},{17,9},{25,17},{1,25},{10,2},{18... | collective-permute-start | bytes 786440 | tf_op jit(solution)/shard_map/ppermute | solution.py:238
  5.2 16.4 %collective-permute-start.4 = (bf16[64,2048]{1,0:T(8,128)(2,1)}, bf16[64,2048]{1,0:T(8,128)(2,1)S(1)}, u32[]{:S(2)}, u32[]{:S(2)}) collective-permute-start(bf16[64,2048]{1,0:T(8,128)(2,1)} %held0), channel_id=1, source_target_pairs={{24,0},{0,8},{8,16},{16,24},{25,1},{1,9},{9,17},{17,25},{26,2},{2,... | collective-permute-start | bytes 786440 | tf_op jit(solution)/shard_map/ppermute | solution.py:238
  5.8 38.4 %copy-start = (bf16[64,2048]{1,0:T(8,128)(2,1)S(1)}, bf16[64,2048]{1,0:T(8,128)(2,1)}, u32[]{:S(2)}) copy-start(bf16[64,2048]{1,0:T(8,128)(2,1)} %held0) | copy-start | bytes 786436
  11.7 5.1 %collective-permute-start = (bf16[384,128]{1,0:T(8,128)(2,1)S(1)}, bf16[384,128]{1,0:T(8,128)(2,1)S(1)}, u32[]{:S(2)}, u32[]{:S(2)}) collective-permute-start(bf16[384,128]{1,0:T(8,128)(2,1)S(1)} %get-tuple-element.14), channel_id=1, source_target_pairs={{0,2},{2,0},{1,3},{3,1},{4,6},{6,4},{5,7},{7,5},{8,10},{10,8},{9,1... | collective-permute-start | bytes 294920 | tf_op jit(solution)/shard_map/ppermute | solution.py:222
  16.7 3.7 %collective-permute-start.1 = (bf16[480,128]{1,0:T(8,128)(2,1)S(1)}, bf16[480,128]{1,0:T(8,128)(2,1)S(1)}, u32[]{:S(2)}, u32[]{:S(2)}) collective-permute-start(bf16[480,128]{1,0:T(8,128)(2,1)S(1)} %get-tuple-element.16), channel_id=1, source_target_pairs={{0,1},{1,0},{2,3},{3,2},{4,5},{5,4},{6,7},{7,6},{8,9},{9,8},{10,11... | collective-permute-start | bytes 368648 | tf_op jit(solution)/shard_map/ppermute | solution.py:222

commit v4 on v3

--- a/solution.py
+++ b/solution.py
@@ -12,8 +12,11 @@
 PROJ = 8192
 LANES = 128
 TENSOR = ("yh", "c")
-GROUP = ("z", "yl")
+GROUP = ("za", "x", "yl")
 PEERS = 16
+RING = 4
+ORDER = (0, 1, 2, 3)
+TILES = 2
 COUNT = 6
 OWN = 192
 HELD = 64
@@ -38,6 +41,11 @@
     return lax.dot_general(a, b, NT, preferred_element_type=f32, precision=precision)
 
 
+def halves(value):
+    high = value.astype(bf16)
+    return high, (value - high.astype(f32)).astype(bf16)
+
+
 def factors(
     act_h, og_h, shr_h, exp_h, sketch_h, ism_h, osm_h, ss_h,
     send, keep,
@@ -52,8 +60,8 @@
         copies[name].start()
 
     start("shr", shr_h, shr)
+    start("sketch", sketch_h, sketch)
     start("ism", ism_h, ism)
-    start("sketch", sketch_h, sketch)
     for i in range(2):
         rows = pl.ds(i * half_rows, half_rows)
         start(f"act{i}", act_h.at[rows], act.at[rows])
@@ -65,23 +73,26 @@
     start("ss", ss_h, ss)
 
     yh = lax.axis_index("yh")
-    for name in ("shr", "ism", "sketch"):
+    for name in ("shr", "sketch", "ism"):
         copies[name].wait()
+    top, rest = halves(sketch[...])
+    low = (sketch[...] - top.astype(f32) - rest.astype(f32)).astype(bf16)
+    fold = dot_nt(jnp.concatenate([top, rest, low], axis=0), shr[...])
+    fold = fold[:32] + fold[32:64] + fold[64:]
+    weights = jnp.concatenate([*halves(fold), ism[...]], axis=0)
     for i in range(2):
         copies[f"act{i}"].wait()
-        block = act[i * half_rows : (i + 1) * half_rows, :]
-        low = dot(block, shr[...])
-        part_a = dot_nt(sketch[...], low, HIGHEST).astype(bf16)
-        part_c = dot_nt(ism[...], block).astype(bf16)
-        for m in range(half_rows // SEQ):
-            n = i * (half_rows // SEQ) + m
-            toks = slice(m * SEQ, (m + 1) * SEQ)
-            for h in range(2):
-                row = OWN + h * PART + n * KROWS
-                for here, mine, other in ((0, part_a, part_c), (1, part_c, part_a)):
-
-                    @pl.when(yh == here)
-                    def _(row=row, h=h, toks=toks, mine=mine, other=other):
+        sums = dot_nt(weights, act[i * half_rows : (i + 1) * half_rows, :])
+        part_a = (sums[:32] + sums[32:64]).astype(bf16)
+        part_c = sums[64:].astype(bf16)
+        for here, mine, other in ((0, part_a, part_c), (1, part_c, part_a)):
+
+            @pl.when(yh == here)
+            def _(i=i, mine=mine, other=other):
+                for m in range(half_rows // SEQ):
+                    toks = slice(m * SEQ, (m + 1) * SEQ)
+                    for h in range(2):
+                        row = OWN + h * PART + (i * (half_rows // SEQ) + m) * KROWS
                         ks = slice(h * KROWS, (h + 1) * KROWS)
                         keep[row : row + KROWS, :] = mine[ks, toks]
                         send[row : row + KROWS, :] = other[ks, toks]
@@ -133,11 +144,12 @@
     place(1 - yh, core, got[:OWN, :])
     place(yh, 1 - core, got2[:OWN, :])
     place(1 - yh, 1 - core, got2[OWN : 2 * OWN, :])
-    left = half[...] + got2[2 * OWN :, :].astype(f32)
+    left = halves((half[...] + got2[2 * OWN :, :].astype(f32)) * (1.0 / SEQ))
     for n in range(COUNT):
         rows = slice(n * KROWS, (n + 1) * KROWS)
-        prod = dot(left[rows], right[n * SEQ : (n + 1) * SEQ, :].astype(f32), HIGHEST)
-        prod = (prod * (1.0 / SEQ)).astype(bf16)
+        pair = jnp.concatenate([term[rows] for term in left], axis=0)
+        prod = dot(pair, right[n * SEQ : (n + 1) * SEQ, :])
+        prod = (prod[:KROWS] + prod[KROWS:]).astype(bf16)
         flat[rows, :] = prod.astype(f32)
         for p in range(PEERS):
             copies[p, rows, :] = prod
@@ -147,16 +159,18 @@
         ].astype(bf16)
 
 
-def inner(got, held0, held1, held2, held3, out, flat, rows_of, held):
-    x = lax.axis_index("x")
-    for r, block in enumerate((held0, held1, held2, held3)):
-        place = lax.rem(x + r, 4)
-        held[pl.ds(pl.multiple_of(place * HELD, HELD), HELD), :] = block[...]
+def inner(*refs):
+    got, *blocks, out, flat, rows_of, held = refs
+    at = 0
+    for block in blocks:
+        size = block.shape[0]
+        held[at : at + size, :] = block[...]
+        at += size
     for p in range(PEERS):
         flat[p * PART : (p + 1) * PART, :] = got[p].astype(f32)
     flat[PEERS * PART :, :] = jnp.zeros((2 * KROWS, LANES), f32)
     train_sq = jnp.zeros((PEERS * 8, LANES), f32)
-    val_sq = jnp.zeros((4 * HELD, LANES), f32)
+    val_sq = jnp.zeros((RING * HELD, LANES), f32)
     for k in range(KROWS):
         lanes = slice(k * LANES, (k + 1) * LANES)
         g = jnp.concatenate(
@@ -175,7 +189,7 @@
     row = lax.broadcasted_iota(jnp.int32, (8, LANES), 0)
     for p in range(PEERS):
         tiles = []
-        for s in range(2):
+        for s in range(TILES):
             lanes = slice(s * LANES, (s + 1) * LANES)
             tile = dots[p * 8 : (p + 1) * 8, lanes]
             tile = jnp.where(row == 6, val_row[:, lanes], tile)
@@ -186,25 +200,25 @@
 
 
 def finish(got, out):
-    place = lax.axis_index("z") * 2 + lax.axis_index("yl")
-
-    def total(z, yl):
-        first = (z * 2 + yl) * 4
-        block = got[first].astype(f32)
+    zb = lax.axis_index("zb")
+    place = (lax.axis_index("za") * 4 + lax.axis_index("x")) * 2 + lax.axis_index("yl")
+
+    def total(peer):
+        block = got[peer * 4].astype(f32)
         for t in range(1, 4):
-            block = block + got[first + t].astype(f32)
+            block = block + got[peer * 4 + t].astype(f32)
         return block
 
     lane = lax.broadcasted_iota(jnp.int32, (8, LANES), 1)
     row = lax.broadcasted_iota(jnp.int32, (8, LANES), 0)
     train = None
-    for z in range(8):
-        pair = [total(z, yl) for yl in range(2)]
+    for plane in range(8):
+        pair = [total(plane * 2 + yl) for yl in range(2)]
         if train is None:
             norm = pair[0][7:8, :] + pair[0][15:16, :]
             mine = jnp.where(lane == place * 8 + row, norm, 0.0)
             train = lax.rsqrt(jnp.sum(mine, axis=1, keepdims=True) + 1e-06) * math.sqrt(PROJ)
-        for s in range(2):
+        for s in range(TILES):
             a, b = (
                 block[s * 8 : (s + 1) * 8, :]
                 * lax.rsqrt(block[s * 8 + 6 : s * 8 + 7, :] + 1e-06)
@@ -214,12 +228,17 @@
             even = jnp.where(lane < HELD, a, pltpu.roll(b, HELD, 1))
             odd = jnp.where(lane < HELD, pltpu.roll(a, HELD, 1), b)
             for q, tile in ((0, even), (1, odd)):
-                at = (z * 4 + s * 2 + q) * LANES
-                out[:, at : at + LANES] = tile[:COUNT]
+                block_zb = lax.rem(zb + ORDER[2 * s + q], RING)
+                at = pl.multiple_of((block_zb * 8 + plane) * LANES, LANES)
+                out[:, pl.ds(at, LANES)] = tile[:COUNT]
 
 
 def swap(value, axis):
     return lax.ppermute(value, axis, [(0, 1), (1, 0)])
+
+
+def from_zb(value, distance):
+    return lax.ppermute(value, "zb", [((i + distance) % RING, i) for i in range(RING)])
 
 
 def on_device(
@@ -234,10 +253,11 @@
     heldout_gradient,
 ):
     shape = jax.ShapeDtypeStruct
-    held = [heldout_gradient] + [
-        lax.ppermute(heldout_gradient, "x", [((i + r) % 4, i) for i in range(4)])
-        for r in (1, 2, 3)
-    ]
+    own = heldout_gradient
+    up = from_zb(own, 1)
+    far = from_zb(own, 2)
+    down = from_zb(own, -1)
+    held = (own, up, far, down)
 
     operands = (
         activations, output_gradient, shrinking_entries, expanding_entries,
@@ -251,6 +271,7 @@
         out_specs=(VMEM, VMEM),
         scratch_shapes=[pltpu.VMEM(v.shape, v.dtype) for v in operands]
         + [pltpu.SemaphoreType.DMA((18,))],
+        cost_estimate=pl.CostEstimate(flops=int(1e9), bytes_accessed=1 << 16, transcendentals=0),
         compiler_params=params(16),
         name="factors",
     )(*(pltpu.with_memory_space_constraint(v, pltpu.HBM) for v in operands))
@@ -260,6 +281,7 @@
         out_shape=(shape((2 * OWN + PART, LANES), bf16), shape((PART, LANES), f32)),
         in_specs=[VMEM] * 2,
         out_specs=(VMEM, VMEM),
+        cost_estimate=pl.CostEstimate(flops=int(0.1e9), bytes_accessed=1 << 16, transcendentals=0),
         compiler_params=params(4),
         name="add_and_pack",
     )(keep, got)
@@ -273,21 +295,26 @@
             pltpu.VMEM((COUNT * SEQ, LANES), bf16),
             pltpu.VMEM((PART, LANES), f32),
         ],
+        cost_estimate=pl.CostEstimate(flops=int(0.1e9), bytes_accessed=1 << 16, transcendentals=0),
         compiler_params=params(4),
         name="products",
     )(keep, got, half, got2)
 
-    copies, *held = lax.optimization_barrier((copies, *held))
-    all_grads = lax.all_to_all(copies, GROUP, 0, 0, tiled=True)
+    all_grads = lax.cond(
+        lax.axis_index("zb") < RING,
+        lambda v: lax.all_to_all(v, GROUP, 0, 0, tiled=True),
+        lambda v: v,
+        copies,
+    )
     blocks = pl.pallas_call(
         inner,
-        out_shape=shape((PEERS * 4, 16, LANES), bf16),
+        out_shape=shape((PEERS * 4, 8 * TILES, LANES), bf16),
         in_specs=[VMEM] * 5,
         out_specs=VMEM,
         scratch_shapes=[
             pltpu.VMEM((PEERS * PART + 2 * KROWS, LANES), f32),
             pltpu.VMEM((PEERS * 8, KROWS * LANES), bf16),
-            pltpu.VMEM((4 * HELD, KROWS * LANES), bf16),
+            pltpu.VMEM((RING * HELD, KROWS * LANES), bf16),
         ],
         compiler_params=params(12),
         name="inner",
@@ -305,8 +332,8 @@
 
 
 def solution(mesh):
-    split = Mesh(mesh.devices.reshape(8, 4, 2, 2, 2), ("z", "x", "yl", "yh", "c"))
-    dp = ("z", "x", "yl")
+    split = Mesh(mesh.devices.reshape(4, 2, 4, 2, 2, 2), ("zb", "za", "x", "yl", "yh", "c"))
+    dp = ("zb", "za", "x", "yl")
     return jax.shard_map(
         on_device,
         mesh=split,

time: 68 us -> 58 us (0.85)
  blocking collectives: 44.2 us -> 30.8 us
  starting transfers between devices: 10.9 us -> 16 us
  Pallas kernels: 9.1 us -> 7.35 us
    all_to_all x1, blocking collectives: 22.6 us -> 13.5 us  [on_device(): lax.all_to_all(v, GROUP, 0, 0, tiled=True)]
    ppermute x3, starting transfers between devices: 5.13 us -> 10.2 us  [from_zb(): lax.ppermute(value, 'zb', [((i + distance) % RING, i) for i in range(RING)])]
    all_to_all x1, blocking collectives: 21.6 us -> 17.3 us  [on_device(): placed = lax.all_to_all(blocks, GROUP + TENSOR, 0, 0, tiled=True)]
    pallas_call x1, Pallas kernels: 5.89 us -> 4.42 us  [on_device(): pl.pallas_call(factors, out_shape=(pack, pack), in_specs=[HBM] * 8, out_s...]
  transfers between devices with their start and end apart: 5 -> 5, of which waited for: 2 -> 2; matrix products, arithmetic and copies ran while one was open for 0% -> 0% of each run, Pallas kernels for 10% -> 9%
where the time goes in v4:
time: 58 us; the launch traced here: 57.9 us
  blocking collectives  30.8 us (53%)
  starting transfers between devices  16 us (28%)
  Pallas kernels  7.35 us (13%)
  waiting for transfers between devices  3.03 us (5%)
  between operations  0.68 us (1%)
    all_to_all x1, blocking collectives, on_device(): placed = lax.all_to_all(blocks, GROUP + TENSOR, 0, 0, tiled=True)  17.3 us
    all_to_all x1, blocking collectives, on_device(): lax.all_to_all(v, GROUP, 0, 0, tiled=True)  13.5 us
    ppermute x3, starting transfers between devices, from_zb(): lax.ppermute(value, 'zb', [((i + distance) % RING, i) for i in range(RING)])  10.2 us
    ppermute x2, starting transfers between devices, swap(): return lax.ppermute(value, axis, [(0, 1), (1, 0)])  5.77 us
    pallas_call x1, Pallas kernels, on_device(): pl.pallas_call(factors, out_shape=(pack, pack), in_specs=[HBM] * 8, out_s...  4.42 us
    ppermute x2, waiting for transfers between devices, swap(): return lax.ppermute(value, axis, [(0, 1), (1, 0)])  3.02 us
    pallas_call x1, Pallas kernels, on_device(): pl.pallas_call(inner, out_shape=shape((PEERS * 4, 8 * TILES, LANES), bf16...  1.21 us
  transfers between devices with their start and end apart: 5, of which 2 were waited for; matrix products, arithmetic and copies ran while one was open for 0% of the time, Pallas kernels for 9%

profile of v4, /device:TPU:1, one launch (start us, length us, event | category | flops | bytes accessed | tf_op | source)
XLA Modules:
  0.0 57.9 jit_solution(10581315407999370117)
XLA Ops:
  0.6 7.8 %collective-permute-start.3 = (bf16[64,2048]{1,0:T(8,128)(2,1)}, bf16[64,2048]{1,0:T(8,128)(2,1)S(1)}, u32[]{:S(2)}, u32[]{:S(2)}) collective-permute-start(bf16[64,2048]{1,0:T(8,128)(2,1)} %refs_1_.1), channel_id=1, source_target_pairs={{128,0},{192,64},{0,128},{64,192},{129,1},{193,65},{1,129},{65,193... | collective-permute-start | bytes 786440 | tf_op jit(solution)/shard_map/ppermute | solution.py:241
  8.5 0.0 collective-permute-start.2
  8.5 2.4 %collective-permute-start.4 = (bf16[64,2048]{1,0:T(8,128)(2,1)}, bf16[64,2048]{1,0:T(8,128)(2,1)S(1)}, u32[]{:S(2)}, u32[]{:S(2)}) collective-permute-start(bf16[64,2048]{1,0:T(8,128)(2,1)} %refs_1_.1), channel_id=1, source_target_pairs={{192,0},{0,64},{64,128},{128,192},{193,1},{1,65},{65,129},{129,193... | collective-permute-start | bytes 786440 | tf_op jit(solution)/shard_map/ppermute | solution.py:241
  10.8 4.4 %factors.1 = (bf16[384,128]{1,0:T(8,128)(2,1)S(1)}, bf16[384,128]{1,0:T(8,128)(2,1)S(1)}) custom-call(bf16[768,1280]{1,0:T(8,128)(2,1)} %act_h.1, bf16[192,5120]{1,0:T(8,128)(2,1)} %og_h.1, bf16[1280,128]{1,0:T(8,128)(2,1)} %shr_h.1, bf16[128,5120]{1,0:T(8,128)(2,1)} %exp_h.1, f32[32,128]{1,0:T(8,128)} %bitcast.3, bf16[32,1280]{1,0:T(8,128)(2,1)} %bitcast.2, ...), custom_call_target="tpu_custom_call" | custom-call | flops 1000000000 | bytes 65536 | tf_op jit(solution)/shard_map/factors/pallas_call | solution.py:267
  15.3 0.0 copy-start
  15.3 3.0 %collective-permute-start = (bf16[384,128]{1,0:T(8,128)(2,1)S(1)}, bf16[384,128]{1,0:T(8,128)(2,1)S(1)}, u32[]{:S(2)}, u32[]{:S(2)}) collective-permute-start(bf16[384,128]{1,0:T(8,128)(2,1)S(1)} %get-tuple-element.14), channel_id=1, source_target_pairs={{0,2},{2,0},{1,3},{3,1},{4,6},{6,4},{5,7},{7,5},{8,10},{10,8},{9,1... | collective-permute-start | bytes 294920 | tf_op jit(solution)/shard_map/ppermute | solution.py:237
  18.3 2.0 %collective-permute-done.got = bf16[384,128]{1,0:T(8,128)(2,1)S(1)} collective-permute-done((bf16[384,128]{1,0:T(8,128)(2,1)S(1)}, bf16[384,128]{1,0:T(8,128)(2,1)S(1)}, u32[]{:S(2)}, u32[]{:S(2)}) %collective-permute-start) | collective-permute-done | bytes 98336 | tf_op jit(solution)/shard_map/ppermute | solution.py:237
  20.3 2.8 %collective-permute-start.1 = (bf16[480,128]{1,0:T(8,128)(2,1)S(1)}, bf16[480,128]{1,0:T(8,128)(2,1)S(1)}, u32[]{:S(2)}, u32[]{:S(2)}) collective-permute-start(bf16[480,128]{1,0:T(8,128)(2,1)S(1)} %get-tuple-element.16), channel_id=1, source_target_pairs={{0,1},{1,0},{2,3},{3,2},{4,5},{5,4},{6,7},{7,6},{8,9},{9,8},{10,11... | collective-permute-start | bytes 368648 | tf_op jit(solution)/shard_map/ppermute | solution.py:237
  23.1 1.0 %collective-permute-done.1.got2 = bf16[480,128]{1,0:T(8,128)(2,1)S(1)} collective-permute-done((bf16[480,128]{1,0:T(8,128)(2,1)S(1)}, bf16[480,128]{1,0:T(8,128)(2,1)S(1)}, u32[]{:S(2)}, u32[]{:S(2)}) %collective-permute-start.1) | collective-permute-done | bytes 122912 | tf_op jit(solution)/shard_map/ppermute | solution.py:237
  24.1 0.8 %products.1 = (bf16[16,96,128]{2,1,0:T(8,128)(2,1)S(1)}, bf16[6,2048]{1,0:T(8,128)(2,1)}) custom-call(bf16[384,128]{1,0:T(8,128)(2,1)S(1)} %get-tuple-element.13.keep, bf16[384,128]{1,0:T(8,128)(2,1)S(1)} %collective-permute-done.got, f32[96,128]{1,0:T(8,128)S(1)} %get-tuple-element.15.half, bf16[480,128]{1,0:T(8,128)(2,1)S(1)} %collective-permute-done.1.got2), custom_call_target="tpu_custom_call" | custom-call | flops 100000000 | bytes 65536 | tf_op jit(solution)/shard_map/products/pallas_call | solution.py:289
  24.9 13.6 %conditional.1 = (bf16[16,96,128]{2,1,0:T(8,128)(2,1)S(1)}) conditional(s32[]{:T(128)} %convert_element_type.3, bf16[16,96,128]{2,1,0:T(8,128)(2,1)S(1)} %get-tuple-element.17, bf16[16,96,128]{2,1,0:T(8,128)(2,1)S(1)} %get-tuple-element.17), branch_computations={%region_0.0_spmd, %region_1.0_spmd} | conditional | bytes 1572872 | solution.py:303
  24.9 13.5 %all_to_all.9 = bf16[16,96,128]{2,1,0:T(8,128)(2,1)S(1)} all-to-all(bf16[16,96,128]{2,1,0:T(8,128)(2,1)S(1)} %copy.13), channel_id=1, replica_groups=mesh['zb'=4,'za'=2,'x'=4,'yl'=2,'yh'=2,'c'=2] {'za','x','yl'}, dimensions={0} | all-to-all | bytes 786432 | tf_op jit(solution)/shard_map/cond/branch_1_fun/all_to_all | solution.py:305
  38.5 0.0 collective-permute-done.3.refs_3_
  38.5 0.0 collective-permute-done.2.refs_2_
  38.5 0.0 collective-permute-done.4.refs_4_
  38.5 0.0 copy-done
  38.5 1.2 %inner.1 = bf16[64,16,128]{2,1,0:T(8,128)(2,1)S(1)} custom-call(bf16[16,96,128]{2,1,0:T(8,128)(2,1)S(1)} %get-tuple-element.19.refs_0_, bf16[64,2048]{1,0:T(8,128)(2,1)S(1)} %copy-done, bf16[64,2048]{1,0:T(8,128)(2,1)S(1)} %collective-permute-done.2.refs_2_, bf16[64,2048]{1,0:T(8,128)(2,1)S(1)} %collective-permute-done.3.refs_3_, ...), custom_call_target="tpu_custom_call" | custom-call | tf_op jit(solution)/shard_map/inner/pallas_call | solution.py:309
  39.7 17.3 %all_to_all.10.got = bf16[64,16,128]{2,1,0:T(8,128)(2,1)S(1)} all-to-all(bf16[64,16,128]{2,1,0:T(8,128)(2,1)S(1)} %inner.1), channel_id=1, replica_groups=mesh['zb'=4,'za'=2,'x'=4,'yl'=2,'yh'=2,'c'=2] {'za','x','yl','yh','c'}, dimensions={0} | all-to-all | bytes 524288 | tf_op jit(solution)/shard_map/all_to_all | solution.py:322
  57.0 0.9 %finish.1 = f32[6,4096]{1,0:T(8,128)} custom-call(bf16[64,16,128]{2,1,0:T(8,128)(2,1)S(1)} %all_to_all.10.got), custom_call_target="tpu_custom_call" | custom-call | tf_op jit(solution)/shard_map/finish/pallas_call | solution.py:323
  (2 shorter events, 0.0 us)
Async XLA Ops:
  0.6 37.8 %collective-permute-start.3 = (bf16[64,2048]{1,0:T(8,128)(2,1)}, bf16[64,2048]{1,0:T(8,128)(2,1)S(1)}, u32[]{:S(2)}, u32[]{:S(2)}) collective-permute-start(bf16[64,2048]{1,0:T(8,128)(2,1)} %refs_1_.1), channel_id=1, source_target_pairs={{128,0},{192,64},{0,128},{64,192},{129,1},{193,65},{1,129},{65,193... | collective-permute-start | bytes 786440 | tf_op jit(solution)/shard_map/ppermute | solution.py:241
  8.5 30.0 %collective-permute-start.2 = (bf16[64,2048]{1,0:T(8,128)(2,1)}, bf16[64,2048]{1,0:T(8,128)(2,1)S(1)}, u32[]{:S(2)}, u32[]{:S(2)}) collective-permute-start(bf16[64,2048]{1,0:T(8,128)(2,1)} %refs_1_.1), channel_id=1, source_target_pairs={{64,0},{128,64},{192,128},{0,192},{65,1},{129,65},{193,129},{1,193... | collective-permute-start | bytes 786440 | tf_op jit(solution)/shard_map/ppermute | solution.py:241
  8.5 30.0 %collective-permute-start.4 = (bf16[64,2048]{1,0:T(8,128)(2,1)}, bf16[64,2048]{1,0:T(8,128)(2,1)S(1)}, u32[]{:S(2)}, u32[]{:S(2)}) collective-permute-start(bf16[64,2048]{1,0:T(8,128)(2,1)} %refs_1_.1), channel_id=1, source_target_pairs={{192,0},{0,64},{64,128},{128,192},{193,1},{1,65},{65,129},{129,193... | collective-permute-start | bytes 786440 | tf_op jit(solution)/shard_map/ppermute | solution.py:241
  15.3 23.2 %copy-start = (bf16[64,2048]{1,0:T(8,128)(2,1)S(1)}, bf16[64,2048]{1,0:T(8,128)(2,1)}, u32[]{:S(2)}) copy-start(bf16[64,2048]{1,0:T(8,128)(2,1)} %refs_1_.1) | copy-start | bytes 786436
  15.3 5.1 %collective-permute-start = (bf16[384,128]{1,0:T(8,128)(2,1)S(1)}, bf16[384,128]{1,0:T(8,128)(2,1)S(1)}, u32[]{:S(2)}, u32[]{:S(2)}) collective-permute-start(bf16[384,128]{1,0:T(8,128)(2,1)S(1)} %get-tuple-element.14), channel_id=1, source_target_pairs={{0,2},{2,0},{1,3},{3,1},{4,6},{6,4},{5,7},{7,5},{8,10},{10,8},{9,1... | collective-permute-start | bytes 294920 | tf_op jit(solution)/shard_map/ppermute | solution.py:237
  20.3 3.7 %collective-permute-start.1 = (bf16[480,128]{1,0:T(8,128)(2,1)S(1)}, bf16[480,128]{1,0:T(8,128)(2,1)S(1)}, u32[]{:S(2)}, u32[]{:S(2)}) collective-permute-start(bf16[480,128]{1,0:T(8,128)(2,1)S(1)} %get-tuple-element.16), channel_id=1, source_target_pairs={{0,1},{1,0},{2,3},{3,2},{4,5},{5,4},{6,7},{7,6},{8,9},{9,8},{10,11... | collective-permute-start | bytes 368648 | tf_op jit(solution)/shard_map/ppermute | solution.py:237

commit v5 on v4

--- a/solution.py
+++ b/solution.py
@@ -12,7 +12,7 @@
 PROJ = 8192
 LANES = 128
 TENSOR = ("yh", "c")
-GROUP = ("za", "x", "yl")
+GROUP = ("yl", "za", "x")
 PEERS = 16
 RING = 4
 ORDER = (0, 1, 2, 3)
@@ -160,32 +160,39 @@
 
 
 def inner(*refs):
-    got, *blocks, out, flat, rows_of, held = refs
+    got, *blocks, out, flat, held = refs
     at = 0
+    squares = []
     for block in blocks:
         size = block.shape[0]
         held[at : at + size, :] = block[...]
         at += size
+        total = jnp.zeros((size, LANES), f32)
+        for k in range(KROWS):
+            h = block[:, k * LANES : (k + 1) * LANES].astype(f32)
+            total = total + h * h
+        squares.append(total)
+    val_sq = jnp.concatenate(squares, axis=0)
     for p in range(PEERS):
         flat[p * PART : (p + 1) * PART, :] = got[p].astype(f32)
     flat[PEERS * PART :, :] = jnp.zeros((2 * KROWS, LANES), f32)
     train_sq = jnp.zeros((PEERS * 8, LANES), f32)
-    val_sq = jnp.zeros((RING * HELD, LANES), f32)
-    for k in range(KROWS):
-        lanes = slice(k * LANES, (k + 1) * LANES)
-        g = jnp.concatenate(
-            [flat[pl.ds(p * PART + k, 8, stride=KROWS), :] for p in range(PEERS)], axis=0
-        )
-        train_sq = train_sq + g * g
-        rows_of[:, lanes] = g.astype(bf16)
-        h = held[:, lanes].astype(f32)
-        val_sq = val_sq + h * h
+    dots = jnp.zeros((PEERS * 8, RING * HELD), f32)
+    for k in range(0, KROWS, 2):
+        pair = []
+        for j in (k, k + 1):
+            g = jnp.concatenate(
+                [flat[pl.ds(p * PART + j, 8, stride=KROWS), :] for p in range(PEERS)], axis=0
+            )
+            train_sq = train_sq + g * g
+            pair.append(g.astype(bf16))
+        lanes = slice(k * LANES, (k + 2) * LANES)
+        dots = dots + dot_nt(jnp.concatenate(pair, axis=1), held[:, lanes])
     ones = jnp.ones((8, LANES), f32)
     train_row = dot_nt(ones, train_sq, HIGHEST)
     val_row = dot_nt(ones, val_sq, HIGHEST)
     high = train_row.astype(bf16).astype(f32)
     norms = (high, train_row - high)
-    dots = dot_nt(rows_of[...], held[...])
     row = lax.broadcasted_iota(jnp.int32, (8, LANES), 0)
     for p in range(PEERS):
         tiles = []
@@ -201,7 +208,7 @@
 
 def finish(got, out):
     zb = lax.axis_index("zb")
-    place = (lax.axis_index("za") * 4 + lax.axis_index("x")) * 2 + lax.axis_index("yl")
+    place = ((lax.axis_index("yl")) * 2 + lax.axis_index("za")) * 4 + lax.axis_index("x")
 
     def total(peer):
         block = got[peer * 4].astype(f32)
@@ -213,7 +220,8 @@
     row = lax.broadcasted_iota(jnp.int32, (8, LANES), 0)
     train = None
     for plane in range(8):
-        pair = [total(plane * 2 + yl) for yl in range(2)]
+        za, x = divmod(plane, 4)
+        pair = [total(((yl) * 2 + za) * 4 + x) for yl in range(2)]
         if train is None:
             norm = pair[0][7:8, :] + pair[0][15:16, :]
             mine = jnp.where(lane == place * 8 + row, norm, 0.0)
@@ -313,7 +321,6 @@
         out_specs=VMEM,
         scratch_shapes=[
             pltpu.VMEM((PEERS * PART + 2 * KROWS, LANES), f32),
-            pltpu.VMEM((PEERS * 8, KROWS * LANES), bf16),
             pltpu.VMEM((RING * HELD, KROWS * LANES), bf16),
         ],
         compiler_params=params(12),

time: 58 us -> 57.3 us (0.988)
    all_to_all x1, blocking collectives: 17.3 us -> 15.6 us  [on_device(): placed = lax.all_to_all(blocks, GROUP + TENSOR, 0, 0, tiled=True)]
    all_to_all x1, blocking collectives: 13.5 us -> 14.8 us  [on_device(): lax.all_to_all(v, GROUP, 0, 0, tiled=True)]
where the time goes in v5:
time: 57.3 us; the launch traced here: 57.2 us
  blocking collectives  30.3 us (53%)
  starting transfers between devices  16 us (28%)
  Pallas kernels  7.14 us (12%)
  waiting for transfers between devices  3.03 us (5%)
  between operations  0.68 us (1%)
    all_to_all x1, blocking collectives, on_device(): placed = lax.all_to_all(blocks, GROUP + TENSOR, 0, 0, tiled=True)  15.6 us
    all_to_all x1, blocking collectives, on_device(): lax.all_to_all(v, GROUP, 0, 0, tiled=True)  14.8 us
    ppermute x3, starting transfers between devices, from_zb(): lax.ppermute(value, 'zb', [((i + distance) % RING, i) for i in range(RING)])  10.2 us
    ppermute x2, starting transfers between devices, swap(): return lax.ppermute(value, axis, [(0, 1), (1, 0)])  5.77 us
    pallas_call x1, Pallas kernels, on_device(): pl.pallas_call(factors, out_shape=(pack, pack), in_specs=[HBM] * 8, out_s...  4.42 us
    ppermute x2, waiting for transfers between devices, swap(): return lax.ppermute(value, axis, [(0, 1), (1, 0)])  3.02 us
  transfers between devices with their start and end apart: 5, of which 2 were waited for; matrix products, arithmetic and copies ran while one was open for 0% of the time, Pallas kernels for 9%

profile of v5, /device:TPU:1, one launch (start us, length us, event | category | flops | bytes accessed | tf_op | source)
XLA Modules:
  0.0 57.2 jit_solution(3663342156294096068)
XLA Ops:
  0.6 7.8 %collective-permute-start.3 = (bf16[64,2048]{1,0:T(8,128)(2,1)}, bf16[64,2048]{1,0:T(8,128)(2,1)S(1)}, u32[]{:S(2)}, u32[]{:S(2)}) collective-permute-start(bf16[64,2048]{1,0:T(8,128)(2,1)} %refs_1_.1), channel_id=1, source_target_pairs={{128,0},{192,64},{0,128},{64,192},{129,1},{193,65},{1,129},{65,193... | collective-permute-start | bytes 786440 | tf_op jit(solution)/shard_map/ppermute | solution.py:249
  8.5 0.0 collective-permute-start.2
  8.5 2.4 %collective-permute-start.4 = (bf16[64,2048]{1,0:T(8,128)(2,1)}, bf16[64,2048]{1,0:T(8,128)(2,1)S(1)}, u32[]{:S(2)}, u32[]{:S(2)}) collective-permute-start(bf16[64,2048]{1,0:T(8,128)(2,1)} %refs_1_.1), channel_id=1, source_target_pairs={{192,0},{0,64},{64,128},{128,192},{193,1},{1,65},{65,129},{129,193... | collective-permute-start | bytes 786440 | tf_op jit(solution)/shard_map/ppermute | solution.py:249
  10.8 4.4 %factors.1 = (bf16[384,128]{1,0:T(8,128)(2,1)S(1)}, bf16[384,128]{1,0:T(8,128)(2,1)S(1)}) custom-call(bf16[768,1280]{1,0:T(8,128)(2,1)} %act_h.1, bf16[192,5120]{1,0:T(8,128)(2,1)} %og_h.1, bf16[1280,128]{1,0:T(8,128)(2,1)} %shr_h.1, bf16[128,5120]{1,0:T(8,128)(2,1)} %exp_h.1, f32[32,128]{1,0:T(8,128)} %bitcast.3, bf16[32,1280]{1,0:T(8,128)(2,1)} %bitcast.2, ...), custom_call_target="tpu_custom_call" | custom-call | flops 1000000000 | bytes 65536 | tf_op jit(solution)/shard_map/factors/pallas_call | solution.py:275
  15.3 0.0 copy-start
  15.3 3.0 %collective-permute-start = (bf16[384,128]{1,0:T(8,128)(2,1)S(1)}, bf16[384,128]{1,0:T(8,128)(2,1)S(1)}, u32[]{:S(2)}, u32[]{:S(2)}) collective-permute-start(bf16[384,128]{1,0:T(8,128)(2,1)S(1)} %get-tuple-element.14), channel_id=1, source_target_pairs={{0,2},{2,0},{1,3},{3,1},{4,6},{6,4},{5,7},{7,5},{8,10},{10,8},{9,1... | collective-permute-start | bytes 294920 | tf_op jit(solution)/shard_map/ppermute | solution.py:245
  18.3 2.0 %collective-permute-done.got = bf16[384,128]{1,0:T(8,128)(2,1)S(1)} collective-permute-done((bf16[384,128]{1,0:T(8,128)(2,1)S(1)}, bf16[384,128]{1,0:T(8,128)(2,1)S(1)}, u32[]{:S(2)}, u32[]{:S(2)}) %collective-permute-start) | collective-permute-done | bytes 98336 | tf_op jit(solution)/shard_map/ppermute | solution.py:245
  20.3 2.8 %collective-permute-start.1 = (bf16[480,128]{1,0:T(8,128)(2,1)S(1)}, bf16[480,128]{1,0:T(8,128)(2,1)S(1)}, u32[]{:S(2)}, u32[]{:S(2)}) collective-permute-start(bf16[480,128]{1,0:T(8,128)(2,1)S(1)} %get-tuple-element.16), channel_id=1, source_target_pairs={{0,1},{1,0},{2,3},{3,2},{4,5},{5,4},{6,7},{7,6},{8,9},{9,8},{10,11... | collective-permute-start | bytes 368648 | tf_op jit(solution)/shard_map/ppermute | solution.py:245
  23.1 1.0 %collective-permute-done.1.got2 = bf16[480,128]{1,0:T(8,128)(2,1)S(1)} collective-permute-done((bf16[480,128]{1,0:T(8,128)(2,1)S(1)}, bf16[480,128]{1,0:T(8,128)(2,1)S(1)}, u32[]{:S(2)}, u32[]{:S(2)}) %collective-permute-start.1) | collective-permute-done | bytes 122912 | tf_op jit(solution)/shard_map/ppermute | solution.py:245
  24.1 0.8 %products.1 = (bf16[16,96,128]{2,1,0:T(8,128)(2,1)S(1)}, bf16[6,2048]{1,0:T(8,128)(2,1)}) custom-call(bf16[384,128]{1,0:T(8,128)(2,1)S(1)} %get-tuple-element.13.keep, bf16[384,128]{1,0:T(8,128)(2,1)S(1)} %collective-permute-done.got, f32[96,128]{1,0:T(8,128)S(1)} %get-tuple-element.15.half, bf16[480,128]{1,0:T(8,128)(2,1)S(1)} %collective-permute-done.1.got2), custom_call_target="tpu_custom_call" | custom-call | flops 100000000 | bytes 65536 | tf_op jit(solution)/shard_map/products/pallas_call | solution.py:297
  24.9 14.8 %conditional.1 = (bf16[16,96,128]{2,1,0:T(8,128)(2,1)S(1)}) conditional(s32[]{:T(128)} %convert_element_type.3, bf16[16,96,128]{2,1,0:T(8,128)(2,1)S(1)} %get-tuple-element.17, bf16[16,96,128]{2,1,0:T(8,128)(2,1)S(1)} %get-tuple-element.17), branch_computations={%region_0.0_spmd, %region_1.0_spmd} | conditional | bytes 1572872 | solution.py:311
  24.9 14.8 %all_to_all.9 = bf16[16,96,128]{2,1,0:T(8,128)(2,1)S(1)} all-to-all(bf16[16,96,128]{2,1,0:T(8,128)(2,1)S(1)} %copy.13), channel_id=1, replica_groups=mesh['zb'=4,'za'=2,'x'=4,'yl'=2,'yh'=2,'c'=2] {'yl','za','x'}, dimensions={0} | all-to-all | bytes 786432 | tf_op jit(solution)/shard_map/cond/branch_1_fun/all_to_all | solution.py:313
  39.7 0.0 collective-permute-done.3.refs_3_
  39.7 0.0 collective-permute-done.2.refs_2_
  39.7 0.0 collective-permute-done.4.refs_4_
  39.7 0.0 copy-done
  39.7 1.0 %inner.1 = bf16[64,16,128]{2,1,0:T(8,128)(2,1)S(1)} custom-call(bf16[16,96,128]{2,1,0:T(8,128)(2,1)S(1)} %get-tuple-element.19.refs_0_, bf16[64,2048]{1,0:T(8,128)(2,1)S(1)} %copy-done, bf16[64,2048]{1,0:T(8,128)(2,1)S(1)} %collective-permute-done.2.refs_2_, bf16[64,2048]{1,0:T(8,128)(2,1)S(1)} %collective-permute-done.3.refs_3_, ...), custom_call_target="tpu_custom_call" | custom-call | tf_op jit(solution)/shard_map/inner/pallas_call | solution.py:317
  40.7 15.6 %all_to_all.10.got = bf16[64,16,128]{2,1,0:T(8,128)(2,1)S(1)} all-to-all(bf16[64,16,128]{2,1,0:T(8,128)(2,1)S(1)} %inner.1), channel_id=1, replica_groups=mesh['zb'=4,'za'=2,'x'=4,'yl'=2,'yh'=2,'c'=2] {'yl','za','x','yh','c'}, dimensions={0} | all-to-all | bytes 524288 | tf_op jit(solution)/shard_map/all_to_all | solution.py:329
  56.3 0.9 %finish.1 = f32[6,4096]{1,0:T(8,128)} custom-call(bf16[64,16,128]{2,1,0:T(8,128)(2,1)S(1)} %all_to_all.10.got), custom_call_target="tpu_custom_call" | custom-call | tf_op jit(solution)/shard_map/finish/pallas_call | solution.py:330
  (2 shorter events, 0.0 us)
Async XLA Ops:
  0.6 39.1 %collective-permute-start.3 = (bf16[64,2048]{1,0:T(8,128)(2,1)}, bf16[64,2048]{1,0:T(8,128)(2,1)S(1)}, u32[]{:S(2)}, u32[]{:S(2)}) collective-permute-start(bf16[64,2048]{1,0:T(8,128)(2,1)} %refs_1_.1), channel_id=1, source_target_pairs={{128,0},{192,64},{0,128},{64,192},{129,1},{193,65},{1,129},{65,193... | collective-permute-start | bytes 786440 | tf_op jit(solution)/shard_map/ppermute | solution.py:249
  8.5 31.2 %collective-permute-start.2 = (bf16[64,2048]{1,0:T(8,128)(2,1)}, bf16[64,2048]{1,0:T(8,128)(2,1)S(1)}, u32[]{:S(2)}, u32[]{:S(2)}) collective-permute-start(bf16[64,2048]{1,0:T(8,128)(2,1)} %refs_1_.1), channel_id=1, source_target_pairs={{64,0},{128,64},{192,128},{0,192},{65,1},{129,65},{193,129},{1,193... | collective-permute-start | bytes 786440 | tf_op jit(solution)/shard_map/ppermute | solution.py:249
  8.5 31.2 %collective-permute-start.4 = (bf16[64,2048]{1,0:T(8,128)(2,1)}, bf16[64,2048]{1,0:T(8,128)(2,1)S(1)}, u32[]{:S(2)}, u32[]{:S(2)}) collective-permute-start(bf16[64,2048]{1,0:T(8,128)(2,1)} %refs_1_.1), channel_id=1, source_target_pairs={{192,0},{0,64},{64,128},{128,192},{193,1},{1,65},{65,129},{129,193... | collective-permute-start | bytes 786440 | tf_op jit(solution)/shard_map/ppermute | solution.py:249
  15.3 24.5 %copy-start = (bf16[64,2048]{1,0:T(8,128)(2,1)S(1)}, bf16[64,2048]{1,0:T(8,128)(2,1)}, u32[]{:S(2)}) copy-start(bf16[64,2048]{1,0:T(8,128)(2,1)} %refs_1_.1) | copy-start | bytes 786436
  15.3 5.1 %collective-permute-start = (bf16[384,128]{1,0:T(8,128)(2,1)S(1)}, bf16[384,128]{1,0:T(8,128)(2,1)S(1)}, u32[]{:S(2)}, u32[]{:S(2)}) collective-permute-start(bf16[384,128]{1,0:T(8,128)(2,1)S(1)} %get-tuple-element.14), channel_id=1, source_target_pairs={{0,2},{2,0},{1,3},{3,1},{4,6},{6,4},{5,7},{7,5},{8,10},{10,8},{9,1... | collective-permute-start | bytes 294920 | tf_op jit(solution)/shard_map/ppermute | solution.py:245
  20.3 3.7 %collective-permute-start.1 = (bf16[480,128]{1,0:T(8,128)(2,1)S(1)}, bf16[480,128]{1,0:T(8,128)(2,1)S(1)}, u32[]{:S(2)}, u32[]{:S(2)}) collective-permute-start(bf16[480,128]{1,0:T(8,128)(2,1)S(1)} %get-tuple-element.16), channel_id=1, source_target_pairs={{0,1},{1,0},{2,3},{3,2},{4,5},{5,4},{6,7},{7,6},{8,9},{9,8},{10,11... | collective-permute-start | bytes 368648 | tf_op jit(solution)/shard_map/ppermute | solution.py:245

commit v6 on v5

--- a/solution.py
+++ b/solution.py
@@ -48,7 +48,7 @@
 
 def factors(
     act_h, og_h, shr_h, exp_h, sketch_h, ism_h, osm_h, ss_h,
-    send, keep,
+    send, keep, own_sums,
     act, og, shr, exp, sketch, ism, osm, ss, sems,
 ):
     half_rows = act.shape[0] // 2
@@ -83,8 +83,8 @@
     for i in range(2):
         copies[f"act{i}"].wait()
         sums = dot_nt(weights, act[i * half_rows : (i + 1) * half_rows, :])
-        part_a = (sums[:32] + sums[32:64]).astype(bf16)
-        part_c = sums[64:].astype(bf16)
+        part_a = sums[:32] + sums[32:64]
+        part_c = sums[64:]
         for here, mine, other in ((0, part_a, part_c), (1, part_c, part_a)):
 
             @pl.when(yh == here)
@@ -92,10 +92,10 @@
                 for m in range(half_rows // SEQ):
                     toks = slice(m * SEQ, (m + 1) * SEQ)
                     for h in range(2):
-                        row = OWN + h * PART + (i * (half_rows // SEQ) + m) * KROWS
+                        row = h * PART + (i * (half_rows // SEQ) + m) * KROWS
                         ks = slice(h * KROWS, (h + 1) * KROWS)
-                        keep[row : row + KROWS, :] = mine[ks, toks]
-                        send[row : row + KROWS, :] = other[ks, toks]
+                        own_sums[row : row + KROWS, :] = mine[ks, toks]
+                        send[OWN + row : OWN + row + KROWS, :] = other[ks, toks].astype(bf16)
 
     e = jnp.zeros((OWN, LANES), f32)
     back = jnp.zeros((OWN, LANES), f32)
@@ -113,16 +113,16 @@
 
         @pl.when(yh == here)
         def _(mine=mine, other=other):
-            keep[:OWN, :] = mine
+            keep[...] = mine
             send[:OWN, :] = other
 
 
-def add_and_pack(keep, got, send, half):
+def add_and_pack(keep, own_sums, got, send, half):
     core = lax.axis_index("c")
-    send[:OWN, :] = keep[:OWN, :]
+    send[:OWN, :] = keep[...]
     send[OWN : 2 * OWN, :] = got[:OWN, :]
     sums = [
-        keep[OWN + h * PART : OWN + (h + 1) * PART, :].astype(f32)
+        own_sums[h * PART : (h + 1) * PART, :]
         + got[OWN + h * PART : OWN + (h + 1) * PART, :].astype(f32)
         for h in range(2)
     ]
@@ -140,7 +140,7 @@
     def place(h, c, value):
         right[pl.ds(pl.multiple_of((h * 2 + c) * OWN, OWN), OWN), :] = value
 
-    place(yh, core, keep[:OWN, :])
+    place(yh, core, keep[...])
     place(1 - yh, core, got[:OWN, :])
     place(yh, 1 - core, got2[:OWN, :])
     place(1 - yh, 1 - core, got2[OWN : 2 * OWN, :])
@@ -272,11 +272,11 @@
         expanding_sketch.T, input_side_matrix.T, output_side_matrix, shrinking_sketch,
     )
     pack = shape((OWN + 2 * PART, LANES), bf16)
-    send, keep = pl.pallas_call(
+    send, keep, own_sums = pl.pallas_call(
         factors,
-        out_shape=(pack, pack),
+        out_shape=(pack, shape((OWN, LANES), bf16), shape((2 * PART, LANES), f32)),
         in_specs=[HBM] * 8,
-        out_specs=(VMEM, VMEM),
+        out_specs=(VMEM,) * 3,
         scratch_shapes=[pltpu.VMEM(v.shape, v.dtype) for v in operands]
         + [pltpu.SemaphoreType.DMA((18,))],
         cost_estimate=pl.CostEstimate(flops=int(1e9), bytes_accessed=1 << 16, transcendentals=0),
@@ -287,12 +287,12 @@
     send2, half = pl.pallas_call(
         add_and_pack,
         out_shape=(shape((2 * OWN + PART, LANES), bf16), shape((PART, LANES), f32)),
-        in_specs=[VMEM] * 2,
+        in_specs=[VMEM] * 3,
         out_specs=(VMEM, VMEM),
         cost_estimate=pl.CostEstimate(flops=int(0.1e9), bytes_accessed=1 << 16, transcendentals=0),
         compiler_params=params(4),
         name="add_and_pack",
-    )(keep, got)
+    )(keep, own_sums, got)
     got2 = swap(send2, "c")
     copies, train_grads = pl.pallas_call(
         products,

time: 57.3 us -> 57.3 us (level)
  no operation moved by 1% of the time
where the time goes in v6:
time: 57.3 us; the launch traced here: 57.2 us
  blocking collectives  30.3 us (53%)
  starting transfers between devices  16 us (28%)
  Pallas kernels  7.14 us (12%)
  waiting for transfers between devices  3.02 us (5%)
  between operations  0.68 us (1%)
    all_to_all x1, blocking collectives, on_device(): placed = lax.all_to_all(blocks, GROUP + TENSOR, 0, 0, tiled=True)  15.6 us
    all_to_all x1, blocking collectives, on_device(): lax.all_to_all(v, GROUP, 0, 0, tiled=True)  14.8 us
    ppermute x3, starting transfers between devices, from_zb(): lax.ppermute(value, 'zb', [((i + distance) % RING, i) for i in range(RING)])  10.2 us
    ppermute x2, starting transfers between devices, swap(): return lax.ppermute(value, axis, [(0, 1), (1, 0)])  5.78 us
    pallas_call x1, Pallas kernels, on_device(): pl.pallas_call(factors, out_shape=(pack, shape((OWN, LANES), bf16), shape...  4.42 us
    ppermute x2, waiting for transfers between devices, swap(): return lax.ppermute(value, axis, [(0, 1), (1, 0)])  3.01 us
  transfers between devices with their start and end apart: 5, of which 2 were waited for; matrix products, arithmetic and copies ran while one was open for 0% of the time, Pallas kernels for 9%

profile of v6, /device:TPU:1, one launch (start us, length us, event | category | flops | bytes accessed | tf_op | source)
XLA Modules:
  0.0 57.2 jit_solution(871394205849894976)
XLA Ops:
  0.6 7.8 %collective-permute-start.3 = (bf16[64,2048]{1,0:T(8,128)(2,1)}, bf16[64,2048]{1,0:T(8,128)(2,1)S(1)}, u32[]{:S(2)}, u32[]{:S(2)}) collective-permute-start(bf16[64,2048]{1,0:T(8,128)(2,1)} %refs_1_.1), channel_id=1, source_target_pairs={{128,0},{192,64},{0,128},{64,192},{129,1},{193,65},{1,129},{65,193... | collective-permute-start | bytes 786440 | tf_op jit(solution)/shard_map/ppermute | solution.py:249
  8.5 0.0 collective-permute-start.2
  8.5 2.4 %collective-permute-start.4 = (bf16[64,2048]{1,0:T(8,128)(2,1)}, bf16[64,2048]{1,0:T(8,128)(2,1)S(1)}, u32[]{:S(2)}, u32[]{:S(2)}) collective-permute-start(bf16[64,2048]{1,0:T(8,128)(2,1)} %refs_1_.1), channel_id=1, source_target_pairs={{192,0},{0,64},{64,128},{128,192},{193,1},{1,65},{65,129},{129,193... | collective-permute-start | bytes 786440 | tf_op jit(solution)/shard_map/ppermute | solution.py:249
  10.8 4.4 %factors.1 = (bf16[384,128]{1,0:T(8,128)(2,1)S(1)}, bf16[192,128]{1,0:T(8,128)(2,1)S(1)}, f32[192,128]{1,0:T(8,128)S(1)}) custom-call(bf16[768,1280]{1,0:T(8,128)(2,1)} %act_h.1, bf16[192,5120]{1,0:T(8,128)(2,1)} %og_h.1, bf16[1280,128]{1,0:T(8,128)(2,1)} %shr_h.1, bf16[128,5120]{1,0:T(8,128)(2,1)} %exp_h.1, f32[32,128]{1,0:T(8,128)} %bitcast.3, ...), custom_call_target="tpu_custom_call" | custom-call | flops 1000000000 | bytes 65536 | tf_op jit(solution)/shard_map/factors/pallas_call | solution.py:275
  15.3 0.0 copy-start
  15.3 3.0 %collective-permute-start = (bf16[384,128]{1,0:T(8,128)(2,1)S(1)}, bf16[384,128]{1,0:T(8,128)(2,1)S(1)}, u32[]{:S(2)}, u32[]{:S(2)}) collective-permute-start(bf16[384,128]{1,0:T(8,128)(2,1)S(1)} %get-tuple-element.15), channel_id=1, source_target_pairs={{0,2},{2,0},{1,3},{3,1},{4,6},{6,4},{5,7},{7,5},{8,10},{10,8},{9,1... | collective-permute-start | bytes 294920 | tf_op jit(solution)/shard_map/ppermute | solution.py:245
  18.3 2.0 %collective-permute-done.got = bf16[384,128]{1,0:T(8,128)(2,1)S(1)} collective-permute-done((bf16[384,128]{1,0:T(8,128)(2,1)S(1)}, bf16[384,128]{1,0:T(8,128)(2,1)S(1)}, u32[]{:S(2)}, u32[]{:S(2)}) %collective-permute-start) | collective-permute-done | bytes 98336 | tf_op jit(solution)/shard_map/ppermute | solution.py:245
  20.3 2.8 %collective-permute-start.1 = (bf16[480,128]{1,0:T(8,128)(2,1)S(1)}, bf16[480,128]{1,0:T(8,128)(2,1)S(1)}, u32[]{:S(2)}, u32[]{:S(2)}) collective-permute-start(bf16[480,128]{1,0:T(8,128)(2,1)S(1)} %get-tuple-element.18), channel_id=1, source_target_pairs={{0,1},{1,0},{2,3},{3,2},{4,5},{5,4},{6,7},{7,6},{8,9},{9,8},{10,11... | collective-permute-start | bytes 368648 | tf_op jit(solution)/shard_map/ppermute | solution.py:245
  23.1 1.0 %collective-permute-done.1.got2 = bf16[480,128]{1,0:T(8,128)(2,1)S(1)} collective-permute-done((bf16[480,128]{1,0:T(8,128)(2,1)S(1)}, bf16[480,128]{1,0:T(8,128)(2,1)S(1)}, u32[]{:S(2)}, u32[]{:S(2)}) %collective-permute-start.1) | collective-permute-done | bytes 122912 | tf_op jit(solution)/shard_map/ppermute | solution.py:245
  24.1 0.8 %products.1 = (bf16[16,96,128]{2,1,0:T(8,128)(2,1)S(1)}, bf16[6,2048]{1,0:T(8,128)(2,1)}) custom-call(bf16[192,128]{1,0:T(8,128)(2,1)S(1)} %get-tuple-element.14.keep, bf16[384,128]{1,0:T(8,128)(2,1)S(1)} %collective-permute-done.got, f32[96,128]{1,0:T(8,128)S(1)} %get-tuple-element.17.half, bf16[480,128]{1,0:T(8,128)(2,1)S(1)} %collective-permute-done.1.got2), custom_call_target="tpu_custom_call" | custom-call | flops 100000000 | bytes 65536 | tf_op jit(solution)/shard_map/products/pallas_call | solution.py:297
  24.9 14.8 %conditional.1 = (bf16[16,96,128]{2,1,0:T(8,128)(2,1)S(1)}) conditional(s32[]{:T(128)} %convert_element_type.3, bf16[16,96,128]{2,1,0:T(8,128)(2,1)S(1)} %get-tuple-element.19, bf16[16,96,128]{2,1,0:T(8,128)(2,1)S(1)} %get-tuple-element.19), branch_computations={%region_0.0_spmd, %region_1.0_spmd} | conditional | bytes 1572872 | solution.py:311
  24.9 14.8 %all_to_all.9 = bf16[16,96,128]{2,1,0:T(8,128)(2,1)S(1)} all-to-all(bf16[16,96,128]{2,1,0:T(8,128)(2,1)S(1)} %copy.13), channel_id=1, replica_groups=mesh['zb'=4,'za'=2,'x'=4,'yl'=2,'yh'=2,'c'=2] {'yl','za','x'}, dimensions={0} | all-to-all | bytes 786432 | tf_op jit(solution)/shard_map/cond/branch_1_fun/all_to_all | solution.py:313
  39.7 0.0 collective-permute-done.3.refs_3_
  39.7 0.0 collective-permute-done.2.refs_2_
  39.7 0.0 collective-permute-done.4.refs_4_
  39.7 0.0 copy-done
  39.7 1.0 %inner.1 = bf16[64,16,128]{2,1,0:T(8,128)(2,1)S(1)} custom-call(bf16[16,96,128]{2,1,0:T(8,128)(2,1)S(1)} %get-tuple-element.21.refs_0_, bf16[64,2048]{1,0:T(8,128)(2,1)S(1)} %copy-done, bf16[64,2048]{1,0:T(8,128)(2,1)S(1)} %collective-permute-done.2.refs_2_, bf16[64,2048]{1,0:T(8,128)(2,1)S(1)} %collective-permute-done.3.refs_3_, ...), custom_call_target="tpu_custom_call" | custom-call | tf_op jit(solution)/shard_map/inner/pallas_call | solution.py:317
  40.7 15.6 %all_to_all.10.got = bf16[64,16,128]{2,1,0:T(8,128)(2,1)S(1)} all-to-all(bf16[64,16,128]{2,1,0:T(8,128)(2,1)S(1)} %inner.1), channel_id=1, replica_groups=mesh['zb'=4,'za'=2,'x'=4,'yl'=2,'yh'=2,'c'=2] {'yl','za','x','yh','c'}, dimensions={0} | all-to-all | bytes 524288 | tf_op jit(solution)/shard_map/all_to_all | solution.py:329
  56.3 0.9 %finish.1 = f32[6,4096]{1,0:T(8,128)} custom-call(bf16[64,16,128]{2,1,0:T(8,128)(2,1)S(1)} %all_to_all.10.got), custom_call_target="tpu_custom_call" | custom-call | tf_op jit(solution)/shard_map/finish/pallas_call | solution.py:330
  (2 shorter events, 0.0 us)
Async XLA Ops:
  0.6 39.1 %collective-permute-start.3 = (bf16[64,2048]{1,0:T(8,128)(2,1)}, bf16[64,2048]{1,0:T(8,128)(2,1)S(1)}, u32[]{:S(2)}, u32[]{:S(2)}) collective-permute-start(bf16[64,2048]{1,0:T(8,128)(2,1)} %refs_1_.1), channel_id=1, source_target_pairs={{128,0},{192,64},{0,128},{64,192},{129,1},{193,65},{1,129},{65,193... | collective-permute-start | bytes 786440 | tf_op jit(solution)/shard_map/ppermute | solution.py:249
  8.5 31.2 %collective-permute-start.2 = (bf16[64,2048]{1,0:T(8,128)(2,1)}, bf16[64,2048]{1,0:T(8,128)(2,1)S(1)}, u32[]{:S(2)}, u32[]{:S(2)}) collective-permute-start(bf16[64,2048]{1,0:T(8,128)(2,1)} %refs_1_.1), channel_id=1, source_target_pairs={{64,0},{128,64},{192,128},{0,192},{65,1},{129,65},{193,129},{1,193... | collective-permute-start | bytes 786440 | tf_op jit(solution)/shard_map/ppermute | solution.py:249
  8.5 31.2 %collective-permute-start.4 = (bf16[64,2048]{1,0:T(8,128)(2,1)}, bf16[64,2048]{1,0:T(8,128)(2,1)S(1)}, u32[]{:S(2)}, u32[]{:S(2)}) collective-permute-start(bf16[64,2048]{1,0:T(8,128)(2,1)} %refs_1_.1), channel_id=1, source_target_pairs={{192,0},{0,64},{64,128},{128,192},{193,1},{1,65},{65,129},{129,193... | collective-permute-start | bytes 786440 | tf_op jit(solution)/shard_map/ppermute | solution.py:249
  15.3 24.5 %copy-start = (bf16[64,2048]{1,0:T(8,128)(2,1)S(1)}, bf16[64,2048]{1,0:T(8,128)(2,1)}, u32[]{:S(2)}) copy-start(bf16[64,2048]{1,0:T(8,128)(2,1)} %refs_1_.1) | copy-start | bytes 786436
  15.3 5.1 %collective-permute-start = (bf16[384,128]{1,0:T(8,128)(2,1)S(1)}, bf16[384,128]{1,0:T(8,128)(2,1)S(1)}, u32[]{:S(2)}, u32[]{:S(2)}) collective-permute-start(bf16[384,128]{1,0:T(8,128)(2,1)S(1)} %get-tuple-element.15), channel_id=1, source_target_pairs={{0,2},{2,0},{1,3},{3,1},{4,6},{6,4},{5,7},{7,5},{8,10},{10,8},{9,1... | collective-permute-start | bytes 294920 | tf_op jit(solution)/shard_map/ppermute | solution.py:245
  20.3 3.7 %collective-permute-start.1 = (bf16[480,128]{1,0:T(8,128)(2,1)S(1)}, bf16[480,128]{1,0:T(8,128)(2,1)S(1)}, u32[]{:S(2)}, u32[]{:S(2)}) collective-permute-start(bf16[480,128]{1,0:T(8,128)(2,1)S(1)} %get-tuple-element.18), channel_id=1, source_target_pairs={{0,1},{1,0},{2,3},{3,2},{4,5},{5,4},{6,7},{7,6},{8,9},{9,8},{10,11... | collective-permute-start | bytes 368648 | tf_op jit(solution)/shard_map/ppermute | solution.py:245

commit v7 on v6

--- a/solution.py
+++ b/solution.py
@@ -15,7 +15,7 @@
 GROUP = ("yl", "za", "x")
 PEERS = 16
 RING = 4
-ORDER = (0, 1, 2, 3)
+ORDER = (0, 2, 3, 1)
 TILES = 2
 COUNT = 6
 OWN = 192
@@ -236,8 +236,9 @@
             even = jnp.where(lane < HELD, a, pltpu.roll(b, HELD, 1))
             odd = jnp.where(lane < HELD, pltpu.roll(a, HELD, 1), b)
             for q, tile in ((0, even), (1, odd)):
-                block_zb = lax.rem(zb + ORDER[2 * s + q], RING)
-                at = pl.multiple_of((block_zb * 8 + plane) * LANES, LANES)
+                away = ORDER[2 * s + q]
+                z = lax.rem(2 * zb + (1 + away if za else 2 * RING - away), 2 * RING)
+                at = pl.multiple_of((z * 4 + x) * LANES, LANES)
                 out[:, pl.ds(at, LANES)] = tile[:COUNT]
 
 
@@ -245,8 +246,13 @@
     return lax.ppermute(value, axis, [(0, 1), (1, 0)])
 
 
-def from_zb(value, distance):
-    return lax.ppermute(value, "zb", [((i + distance) % RING, i) for i in range(RING)])
+def from_side(value, distance):
+    planes = 2 * RING
+    return lax.ppermute(
+        value,
+        ("zb", "za"),
+        [((i + (distance if i % 2 else -distance)) % planes, i) for i in range(planes)],
+    )
 
 
 def on_device(
@@ -262,10 +268,10 @@
 ):
     shape = jax.ShapeDtypeStruct
     own = heldout_gradient
-    up = from_zb(own, 1)
-    far = from_zb(own, 2)
-    down = from_zb(own, -1)
-    held = (own, up, far, down)
+    middle = from_side(own, 2)
+    far = from_side(own, 3)
+    near = from_side(own, 1)
+    held = (own, middle, far, near)
 
     operands = (
         activations, output_gradient, shrinking_entries, expanding_entries,

time: 57.3 us -> 55 us (0.960)
  starting transfers between devices: 16 us -> 13.8 us
    ppermute x3, starting transfers between devices: 10.2 us -> 8.58 us  [from_side(): lax.ppermute(value, ('zb', 'za'), [((i + (distance if i % 2 else -distanc...]
    all_to_all x1, blocking collectives: 14.8 us -> 13.9 us  [on_device(): lax.all_to_all(v, GROUP, 0, 0, tiled=True)]
    ppermute x2, starting transfers between devices: 5.78 us -> 5.2 us  [swap(): return lax.ppermute(value, axis, [(0, 1), (1, 0)])]
  transfers between devices with their start and end apart: 5 -> 5, of which waited for: 2 -> 2; matrix products, arithmetic and copies ran while one was open for 0% -> 0% of each run, Pallas kernels for 9% -> 10%
where the time goes in v7:
time: 55 us; the launch traced here: 54.8 us
  blocking collectives  29.9 us (54%)
  starting transfers between devices  13.8 us (25%)
  Pallas kernels  7.14 us (13%)
  waiting for transfers between devices  3.32 us (6%)
  between operations  0.68 us (1%)
    all_to_all x1, blocking collectives, on_device(): placed = lax.all_to_all(blocks, GROUP + TENSOR, 0, 0, tiled=True)  16 us
    all_to_all x1, blocking collectives, on_device(): lax.all_to_all(v, GROUP, 0, 0, tiled=True)  13.9 us
    ppermute x3, starting transfers between devices, from_side(): lax.ppermute(value, ('zb', 'za'), [((i + (distance if i % 2 else -distanc...  8.58 us
    ppermute x2, starting transfers between devices, swap(): return lax.ppermute(value, axis, [(0, 1), (1, 0)])  5.2 us
    pallas_call x1, Pallas kernels, on_device(): pl.pallas_call(factors, out_shape=(pack, shape((OWN, LANES), bf16), shape...  4.42 us
    ppermute x2, waiting for transfers between devices, swap(): return lax.ppermute(value, axis, [(0, 1), (1, 0)])  3.31 us
  transfers between devices with their start and end apart: 5, of which 2 were waited for; matrix products, arithmetic and copies ran while one was open for 0% of the time, Pallas kernels for 10%

profile of v7, /device:TPU:1, one launch (start us, length us, event | category | flops | bytes accessed | tf_op | source)
XLA Modules:
  0.0 54.8 jit_solution(11911969841200882365)
XLA Ops:
  0.6 7.4 %collective-permute-start.3 = (bf16[64,2048]{1,0:T(8,128)(2,1)}, bf16[64,2048]{1,0:T(8,128)(2,1)S(1)}, u32[]{:S(2)}, u32[]{:S(2)}) collective-permute-start(bf16[64,2048]{1,0:T(8,128)(2,1)} %refs_1_.1), channel_id=1, source_target_pairs={{160,0},{128,32},{224,64},{192,96},{32,128},{0,160},{96,192},{64,2... | collective-permute-start | bytes 786440 | tf_op jit(solution)/shard_map/ppermute | solution.py:251
  8.0 1.2 %collective-permute-start.2 = (bf16[64,2048]{1,0:T(8,128)(2,1)}, bf16[64,2048]{1,0:T(8,128)(2,1)S(1)}, u32[]{:S(2)}, u32[]{:S(2)}) collective-permute-start(bf16[64,2048]{1,0:T(8,128)(2,1)} %refs_1_.1), channel_id=1, source_target_pairs={{192,0},{96,32},{0,64},{160,96},{64,128},{224,160},{128,192},{32,2... | collective-permute-start | bytes 786440 | tf_op jit(solution)/shard_map/ppermute | solution.py:251
  9.2 0.0 collective-permute-start.4
  9.2 4.4 %factors.1 = (bf16[384,128]{1,0:T(8,128)(2,1)S(1)}, bf16[192,128]{1,0:T(8,128)(2,1)S(1)}, f32[192,128]{1,0:T(8,128)S(1)}) custom-call(bf16[768,1280]{1,0:T(8,128)(2,1)} %act_h.1, bf16[192,5120]{1,0:T(8,128)(2,1)} %og_h.1, bf16[1280,128]{1,0:T(8,128)(2,1)} %shr_h.1, bf16[128,5120]{1,0:T(8,128)(2,1)} %exp_h.1, f32[32,128]{1,0:T(8,128)} %bitcast.3, ...), custom_call_target="tpu_custom_call" | custom-call | flops 1000000000 | bytes 65536 | tf_op jit(solution)/shard_map/factors/pallas_call | solution.py:281
  13.6 0.0 copy-start
  13.7 3.0 %collective-permute-start = (bf16[384,128]{1,0:T(8,128)(2,1)S(1)}, bf16[384,128]{1,0:T(8,128)(2,1)S(1)}, u32[]{:S(2)}, u32[]{:S(2)}) collective-permute-start(bf16[384,128]{1,0:T(8,128)(2,1)S(1)} %get-tuple-element.15), channel_id=1, source_target_pairs={{0,2},{2,0},{1,3},{3,1},{4,6},{6,4},{5,7},{7,5},{8,10},{10,8},{9,1... | collective-permute-start | bytes 294920 | tf_op jit(solution)/shard_map/ppermute | solution.py:246
  16.7 2.3 %collective-permute-done.got = bf16[384,128]{1,0:T(8,128)(2,1)S(1)} collective-permute-done((bf16[384,128]{1,0:T(8,128)(2,1)S(1)}, bf16[384,128]{1,0:T(8,128)(2,1)S(1)}, u32[]{:S(2)}, u32[]{:S(2)}) %collective-permute-start) | collective-permute-done | bytes 98336 | tf_op jit(solution)/shard_map/ppermute | solution.py:246
  19.0 2.2 %collective-permute-start.1 = (bf16[480,128]{1,0:T(8,128)(2,1)S(1)}, bf16[480,128]{1,0:T(8,128)(2,1)S(1)}, u32[]{:S(2)}, u32[]{:S(2)}) collective-permute-start(bf16[480,128]{1,0:T(8,128)(2,1)S(1)} %get-tuple-element.18), channel_id=1, source_target_pairs={{0,1},{1,0},{2,3},{3,2},{4,5},{5,4},{6,7},{7,6},{8,9},{9,8},{10,11... | collective-permute-start | bytes 368648 | tf_op jit(solution)/shard_map/ppermute | solution.py:246
  21.2 1.0 %collective-permute-done.1.got2 = bf16[480,128]{1,0:T(8,128)(2,1)S(1)} collective-permute-done((bf16[480,128]{1,0:T(8,128)(2,1)S(1)}, bf16[480,128]{1,0:T(8,128)(2,1)S(1)}, u32[]{:S(2)}, u32[]{:S(2)}) %collective-permute-start.1) | collective-permute-done | bytes 122912 | tf_op jit(solution)/shard_map/ppermute | solution.py:246
  22.2 0.8 %products.1 = (bf16[16,96,128]{2,1,0:T(8,128)(2,1)S(1)}, bf16[6,2048]{1,0:T(8,128)(2,1)}) custom-call(bf16[192,128]{1,0:T(8,128)(2,1)S(1)} %get-tuple-element.14.keep, bf16[384,128]{1,0:T(8,128)(2,1)S(1)} %collective-permute-done.got, f32[96,128]{1,0:T(8,128)S(1)} %get-tuple-element.17.half, bf16[480,128]{1,0:T(8,128)(2,1)S(1)} %collective-permute-done.1.got2), custom_call_target="tpu_custom_call" | custom-call | flops 100000000 | bytes 65536 | tf_op jit(solution)/shard_map/products/pallas_call | solution.py:303
  23.0 13.9 %conditional.1 = (bf16[16,96,128]{2,1,0:T(8,128)(2,1)S(1)}) conditional(s32[]{:T(128)} %convert_element_type.3, bf16[16,96,128]{2,1,0:T(8,128)(2,1)S(1)} %get-tuple-element.19, bf16[16,96,128]{2,1,0:T(8,128)(2,1)S(1)} %get-tuple-element.19), branch_computations={%region_0.0_spmd, %region_1.0_spmd} | conditional | bytes 1572872 | solution.py:317
  23.0 13.9 %all_to_all.9 = bf16[16,96,128]{2,1,0:T(8,128)(2,1)S(1)} all-to-all(bf16[16,96,128]{2,1,0:T(8,128)(2,1)S(1)} %copy.13), channel_id=1, replica_groups=mesh['zb'=4,'za'=2,'x'=4,'yl'=2,'yh'=2,'c'=2] {'yl','za','x'}, dimensions={0} | all-to-all | bytes 786432 | tf_op jit(solution)/shard_map/cond/branch_1_fun/all_to_all | solution.py:319
  36.9 0.0 collective-permute-done.3.refs_3_
  36.9 0.0 collective-permute-done.2.refs_2_
  36.9 0.0 collective-permute-done.4.refs_4_
  36.9 0.0 copy-done
  36.9 1.0 %inner.1 = bf16[64,16,128]{2,1,0:T(8,128)(2,1)S(1)} custom-call(bf16[16,96,128]{2,1,0:T(8,128)(2,1)S(1)} %get-tuple-element.21.refs_0_, bf16[64,2048]{1,0:T(8,128)(2,1)S(1)} %copy-done, bf16[64,2048]{1,0:T(8,128)(2,1)S(1)} %collective-permute-done.2.refs_2_, bf16[64,2048]{1,0:T(8,128)(2,1)S(1)} %collective-permute-done.3.refs_3_, ...), custom_call_target="tpu_custom_call" | custom-call | tf_op jit(solution)/shard_map/inner/pallas_call | solution.py:323
  37.9 16.0 %all_to_all.10.got = bf16[64,16,128]{2,1,0:T(8,128)(2,1)S(1)} all-to-all(bf16[64,16,128]{2,1,0:T(8,128)(2,1)S(1)} %inner.1), channel_id=1, replica_groups=mesh['zb'=4,'za'=2,'x'=4,'yl'=2,'yh'=2,'c'=2] {'yl','za','x','yh','c'}, dimensions={0} | all-to-all | bytes 524288 | tf_op jit(solution)/shard_map/all_to_all | solution.py:335
  53.9 0.9 %finish.1 = f32[6,4096]{1,0:T(8,128)} custom-call(bf16[64,16,128]{2,1,0:T(8,128)(2,1)S(1)} %all_to_all.10.got), custom_call_target="tpu_custom_call" | custom-call | tf_op jit(solution)/shard_map/finish/pallas_call | solution.py:336
  (2 shorter events, 0.0 us)
Async XLA Ops:
  0.6 36.3 %collective-permute-start.3 = (bf16[64,2048]{1,0:T(8,128)(2,1)}, bf16[64,2048]{1,0:T(8,128)(2,1)S(1)}, u32[]{:S(2)}, u32[]{:S(2)}) collective-permute-start(bf16[64,2048]{1,0:T(8,128)(2,1)} %refs_1_.1), channel_id=1, source_target_pairs={{160,0},{128,32},{224,64},{192,96},{32,128},{0,160},{96,192},{64,2... | collective-permute-start | bytes 786440 | tf_op jit(solution)/shard_map/ppermute | solution.py:251
  8.0 28.9 %collective-permute-start.2 = (bf16[64,2048]{1,0:T(8,128)(2,1)}, bf16[64,2048]{1,0:T(8,128)(2,1)S(1)}, u32[]{:S(2)}, u32[]{:S(2)}) collective-permute-start(bf16[64,2048]{1,0:T(8,128)(2,1)} %refs_1_.1), channel_id=1, source_target_pairs={{192,0},{96,32},{0,64},{160,96},{64,128},{224,160},{128,192},{32,2... | collective-permute-start | bytes 786440 | tf_op jit(solution)/shard_map/ppermute | solution.py:251
  9.2 27.7 %collective-permute-start.4 = (bf16[64,2048]{1,0:T(8,128)(2,1)}, bf16[64,2048]{1,0:T(8,128)(2,1)S(1)}, u32[]{:S(2)}, u32[]{:S(2)}) collective-permute-start(bf16[64,2048]{1,0:T(8,128)(2,1)} %refs_1_.1), channel_id=1, source_target_pairs={{224,0},{64,32},{32,64},{128,96},{96,128},{192,160},{160,192},{0,2... | collective-permute-start | bytes 786440 | tf_op jit(solution)/shard_map/ppermute | solution.py:251
  13.6 23.3 %copy-start = (bf16[64,2048]{1,0:T(8,128)(2,1)S(1)}, bf16[64,2048]{1,0:T(8,128)(2,1)}, u32[]{:S(2)}) copy-start(bf16[64,2048]{1,0:T(8,128)(2,1)} %refs_1_.1) | copy-start | bytes 786436
  13.7 5.4 %collective-permute-start = (bf16[384,128]{1,0:T(8,128)(2,1)S(1)}, bf16[384,128]{1,0:T(8,128)(2,1)S(1)}, u32[]{:S(2)}, u32[]{:S(2)}) collective-permute-start(bf16[384,128]{1,0:T(8,128)(2,1)S(1)} %get-tuple-element.15), channel_id=1, source_target_pairs={{0,2},{2,0},{1,3},{3,1},{4,6},{6,4},{5,7},{7,5},{8,10},{10,8},{9,1... | collective-permute-start | bytes 294920 | tf_op jit(solution)/shard_map/ppermute | solution.py:246
  19.0 3.2 %collective-permute-start.1 = (bf16[480,128]{1,0:T(8,128)(2,1)S(1)}, bf16[480,128]{1,0:T(8,128)(2,1)S(1)}, u32[]{:S(2)}, u32[]{:S(2)}) collective-permute-start(bf16[480,128]{1,0:T(8,128)(2,1)S(1)} %get-tuple-element.18), channel_id=1, source_target_pairs={{0,1},{1,0},{2,3},{3,2},{4,5},{5,4},{6,7},{7,6},{8,9},{9,8},{10,11... | collective-permute-start | bytes 368648 | tf_op jit(solution)/shard_map/ppermute | solution.py:246

commit v8 on v7

--- a/solution.py
+++ b/solution.py
@@ -15,7 +15,8 @@
 GROUP = ("yl", "za", "x")
 PEERS = 16
 RING = 4
-ORDER = (0, 2, 3, 1)
+ORDER = (0, 1, 2, 3)
+EARLY_INPUT, EARLY_OUTPUT = 3, 2
 TILES = 2
 COUNT = 6
 OWN = 192
@@ -46,75 +47,90 @@
     return high, (value - high.astype(f32)).astype(bf16)
 
 
-def factors(
-    act_h, og_h, shr_h, exp_h, sketch_h, ism_h, osm_h, ss_h,
-    send, keep, own_sums,
-    act, og, shr, exp, sketch, ism, osm, ss, sems,
-):
+def factors(turn, *refs):
+    act_h, og_h, shr_h, exp_h, sketch_h, ism_h, osm_h, ss_h = refs[:8]
+    send, keep, own_sums, act, og, shr, exp, sketch, ism, osm, ss, sems = refs[-12:]
     half_rows = act.shape[0] // 2
     depth = og.shape[1] // 4
+    z = lax.axis_index("zb") * 2 + lax.axis_index("za")
+    yh = lax.axis_index("yh")
+    do_input, do_output = (z < EARLY_INPUT, z < EARLY_OUTPUT) if turn == 0 else (z >= EARLY_INPUT, z >= EARLY_OUTPUT)
     copies = {}
 
-    def start(name, src, dst):
+    def copy(name, src, dst):
         copies[name] = pltpu.make_async_copy(src, dst, sems.at[len(copies)])
-        copies[name].start()
-
-    start("shr", shr_h, shr)
-    start("sketch", sketch_h, sketch)
-    start("ism", ism_h, ism)
+
+    copy("shr", shr_h, shr)
+    copy("sketch", sketch_h, sketch)
+    copy("ism", ism_h, ism)
     for i in range(2):
         rows = pl.ds(i * half_rows, half_rows)
-        start(f"act{i}", act_h.at[rows], act.at[rows])
+        copy(f"act{i}", act_h.at[rows], act.at[rows])
+    inputs = list(copies)
     for i in range(4):
         cols = pl.ds(i * depth, depth)
-        start(f"og{i}", og_h.at[:, cols], og.at[:, cols])
-        start(f"osm{i}", osm_h.at[cols], osm.at[cols])
-        start(f"exp{i}", exp_h.at[:, cols], exp.at[:, cols])
-    start("ss", ss_h, ss)
-
-    yh = lax.axis_index("yh")
-    for name in ("shr", "sketch", "ism"):
-        copies[name].wait()
-    top, rest = halves(sketch[...])
-    low = (sketch[...] - top.astype(f32) - rest.astype(f32)).astype(bf16)
-    fold = dot_nt(jnp.concatenate([top, rest, low], axis=0), shr[...])
-    fold = fold[:32] + fold[32:64] + fold[64:]
-    weights = jnp.concatenate([*halves(fold), ism[...]], axis=0)
-    for i in range(2):
-        copies[f"act{i}"].wait()
-        sums = dot_nt(weights, act[i * half_rows : (i + 1) * half_rows, :])
-        part_a = sums[:32] + sums[32:64]
-        part_c = sums[64:]
-        for here, mine, other in ((0, part_a, part_c), (1, part_c, part_a)):
+        copy(f"og{i}", og_h.at[:, cols], og.at[:, cols])
+        copy(f"osm{i}", osm_h.at[cols], osm.at[cols])
+        copy(f"exp{i}", exp_h.at[:, cols], exp.at[:, cols])
+    copy("ss", ss_h, ss)
+
+    @pl.when(do_input)
+    def _():
+        for name in inputs:
+            copies[name].start()
+
+    @pl.when(do_output)
+    def _():
+        for name in copies:
+            if name not in inputs:
+                copies[name].start()
+
+    @pl.when(do_input)
+    def _():
+        for name in ("shr", "sketch", "ism"):
+            copies[name].wait()
+        top, rest = halves(sketch[...])
+        low = (sketch[...] - top.astype(f32) - rest.astype(f32)).astype(bf16)
+        fold = dot_nt(jnp.concatenate([top, rest, low], axis=0), shr[...])
+        fold = fold[:32] + fold[32:64] + fold[64:]
+        weights = jnp.concatenate([*halves(fold), ism[...]], axis=0)
+        for i in range(2):
+            copies[f"act{i}"].wait()
+            sums = dot_nt(weights, act[i * half_rows : (i + 1) * half_rows, :])
+            part_a = sums[:32] + sums[32:64]
+            part_c = sums[64:]
+            for here, mine, other in ((0, part_a, part_c), (1, part_c, part_a)):
+
+                @pl.when(yh == here)
+                def _(i=i, mine=mine, other=other):
+                    for m in range(half_rows // SEQ):
+                        toks = slice(m * SEQ, (m + 1) * SEQ)
+                        for h in range(2):
+                            row = h * PART + (i * (half_rows // SEQ) + m) * KROWS
+                            ks = slice(h * KROWS, (h + 1) * KROWS)
+                            own_sums[row : row + KROWS, :] = mine[ks, toks]
+                            send[OWN + row : OWN + row + KROWS, :] = other[ks, toks].astype(bf16)
+
+    @pl.when(do_output)
+    def _():
+        e = jnp.zeros((OWN, LANES), f32)
+        back = jnp.zeros((OWN, LANES), f32)
+        for i in range(4):
+            cols = slice(i * depth, (i + 1) * depth)
+            for name in ("og", "osm", "exp"):
+                copies[f"{name}{i}"].wait()
+            block = og[:, cols]
+            e = e + dot(block, osm[cols, :])
+            back = back + dot_nt(block, exp[:, cols])
+        copies["ss"].wait()
+        e = e.astype(bf16)
+        f = dot(back.astype(bf16), ss[...]).astype(bf16)
+        for here, mine, other in ((0, e, f), (1, f, e)):
 
             @pl.when(yh == here)
-            def _(i=i, mine=mine, other=other):
-                for m in range(half_rows // SEQ):
-                    toks = slice(m * SEQ, (m + 1) * SEQ)
-                    for h in range(2):
-                        row = h * PART + (i * (half_rows // SEQ) + m) * KROWS
-                        ks = slice(h * KROWS, (h + 1) * KROWS)
-                        own_sums[row : row + KROWS, :] = mine[ks, toks]
-                        send[OWN + row : OWN + row + KROWS, :] = other[ks, toks].astype(bf16)
-
-    e = jnp.zeros((OWN, LANES), f32)
-    back = jnp.zeros((OWN, LANES), f32)
-    for i in range(4):
-        cols = slice(i * depth, (i + 1) * depth)
-        for name in ("og", "osm", "exp"):
-            copies[f"{name}{i}"].wait()
-        block = og[:, cols]
-        e = e + dot(block, osm[cols, :])
-        back = back + dot_nt(block, exp[:, cols])
-    copies["ss"].wait()
-    e = e.astype(bf16)
-    f = dot(back.astype(bf16), ss[...]).astype(bf16)
-    for here, mine, other in ((0, e, f), (1, f, e)):
-
-        @pl.when(yh == here)
-        def _(mine=mine, other=other):
-            keep[...] = mine
-            send[:OWN, :] = other
+            def _(mine=mine, other=other):
+                keep[...] = mine
+                send[:OWN, :] = other
 
 
 def add_and_pack(keep, own_sums, got, send, half):
@@ -268,27 +284,35 @@
 ):
     shape = jax.ShapeDtypeStruct
     own = heldout_gradient
-    middle = from_side(own, 2)
-    far = from_side(own, 3)
-    near = from_side(own, 1)
-    held = (own, middle, far, near)
-
     operands = (
         activations, output_gradient, shrinking_entries, expanding_entries,
         expanding_sketch.T, input_side_matrix.T, output_side_matrix, shrinking_sketch,
     )
     pack = shape((OWN + 2 * PART, LANES), bf16)
-    send, keep, own_sums = pl.pallas_call(
-        factors,
-        out_shape=(pack, shape((OWN, LANES), bf16), shape((2 * PART, LANES), f32)),
-        in_specs=[HBM] * 8,
-        out_specs=(VMEM,) * 3,
-        scratch_shapes=[pltpu.VMEM(v.shape, v.dtype) for v in operands]
-        + [pltpu.SemaphoreType.DMA((18,))],
-        cost_estimate=pl.CostEstimate(flops=int(1e9), bytes_accessed=1 << 16, transcendentals=0),
-        compiler_params=params(16),
-        name="factors",
-    )(*(pltpu.with_memory_space_constraint(v, pltpu.HBM) for v in operands))
+    shapes = operands
+    operands = [pltpu.with_memory_space_constraint(v, pltpu.HBM) for v in operands]
+
+    def work(turn, *before):
+        return pl.pallas_call(
+            functools.partial(factors, turn),
+            out_shape=(pack, shape((OWN, LANES), bf16), shape((2 * PART, LANES), f32)),
+            in_specs=[HBM] * 8 + [VMEM] * len(before),
+            out_specs=(VMEM,) * 3,
+            input_output_aliases={8: 0, 9: 1, 10: 2} if before else {},
+            scratch_shapes=[pltpu.VMEM(v.shape, v.dtype) for v in shapes]
+            + [pltpu.SemaphoreType.DMA((18,))],
+            cost_estimate=pl.CostEstimate(flops=int(1e9), bytes_accessed=1 << 16, transcendentals=0),
+            compiler_params=params(16),
+            name=f"factors_{turn}",
+        )(*operands, *before)
+
+    send, keep, own_sums = work(0)
+    own, keep = lax.optimization_barrier((own, keep))
+    near = from_side(own, 1)
+    middle = from_side(own, 2)
+    far = from_side(own, 3)
+    held = (own, near, middle, far)
+    send, keep, own_sums = work(1, send, keep, own_sums)
     got = swap(send, "yh")
     send2, half = pl.pallas_call(
         add_and_pack,

time: 55 us -> 54.2 us (0.985)
  starting transfers between devices: 13.8 us -> 12.9 us
    ppermute x3, starting transfers between devices: 8.58 us -> 5.12 us  [from_side(): lax.ppermute(value, ('zb', 'za'), [((i + (distance if i % 2 else -distanc...]
    ppermute x2, starting transfers between devices: 5.2 us -> 7.79 us  [swap(): return lax.ppermute(value, axis, [(0, 1), (1, 0)])]
    pallas_call x1 -> x2, Pallas kernels: 4.42 us -> 4.45 us  [work(): pl.pallas_call(functools.partial(factors, turn), out_shape=(pack, shape((...]
  transfers between devices with their start and end apart: 5 -> 5, of which waited for: 2 -> 2; matrix products, arithmetic and copies ran while one was open for 0% -> 0% of each run, Pallas kernels for 10% -> 2%
where the time goes in v8:
time: 54.2 us; the launch traced here: 53.6 us
  blocking collectives  29.5 us (54%)
  starting transfers between devices  12.9 us (24%)
  Pallas kernels  7.17 us (13%)
  waiting for transfers between devices  3.29 us (6%)
  between operations  0.68 us (1%)
    all_to_all x1, blocking collectives, on_device(): placed = lax.all_to_all(blocks, GROUP + TENSOR, 0, 0, tiled=True)  16 us
    all_to_all x1, blocking collectives, on_device(): lax.all_to_all(v, GROUP, 0, 0, tiled=True)  13.5 us
    ppermute x2, starting transfers between devices, swap(): return lax.ppermute(value, axis, [(0, 1), (1, 0)])  7.79 us
    ppermute x3, starting transfers between devices, from_side(): lax.ppermute(value, ('zb', 'za'), [((i + (distance if i % 2 else -distanc...  5.12 us
    pallas_call x2, Pallas kernels, work(): pl.pallas_call(functools.partial(factors, turn), out_shape=(pack, shape((...  4.45 us
    ppermute x2, waiting for transfers between devices, swap(): return lax.ppermute(value, axis, [(0, 1), (1, 0)])  3.28 us
  transfers between devices with their start and end apart: 5, of which 2 were waited for; matrix products, arithmetic and copies ran while one was open for 0% of the time, Pallas kernels for 2%

profile of v8, /device:TPU:1, one launch (start us, length us, event | category | flops | bytes accessed | tf_op | source)
XLA Modules:
  0.0 53.6 jit_solution(12609947385032461871)
XLA Ops:
  0.6 0.0 copy-start
  0.6 4.3 %factors_0.1 = (bf16[384,128]{1,0:T(8,128)(2,1)S(1)}, bf16[192,128]{1,0:T(8,128)(2,1)S(1)}, f32[192,128]{1,0:T(8,128)S(1)}) custom-call(bf16[768,1280]{1,0:T(8,128)(2,1)} %refs_0_.3, bf16[192,5120]{1,0:T(8,128)(2,1)} %refs_1_.3, bf16[1280,128]{1,0:T(8,128)(2,1)} %refs_2_.3, bf16[128,5120]{1,0:T(8,128)(2,1)} %refs_3_.3, f32[32,128]{1,0:T(8,128)} %bitcast.4, ...), custom_call_target="tpu_custom_call" | custom-call | flops 1000000000 | bytes 65536 | tf_op jit(solution)/shard_map/factors_0/pallas_call | solution.py:296
  4.9 0.0 copy-done
  4.9 3.9 %collective-permute-start.4 = (bf16[64,2048]{1,0:T(8,128)(2,1)S(1)}, bf16[64,2048]{1,0:T(8,128)(2,1)S(1)}, u32[]{:S(2)}, u32[]{:S(2)}) collective-permute-start(bf16[64,2048]{1,0:T(8,128)(2,1)S(1)} %copy-done), channel_id=1, source_target_pairs={{160,0},{128,32},{224,64},{192,96},{32,128},{0,160},{96,192},{64,2... | collective-permute-start | bytes 786440 | tf_op jit(solution)/shard_map/ppermute | solution.py:267
  8.9 1.2 %collective-permute-start.3 = (bf16[64,2048]{1,0:T(8,128)(2,1)S(1)}, bf16[64,2048]{1,0:T(8,128)(2,1)S(1)}, u32[]{:S(2)}, u32[]{:S(2)}) collective-permute-start(bf16[64,2048]{1,0:T(8,128)(2,1)S(1)} %copy-done), channel_id=1, source_target_pairs={{192,0},{96,32},{0,64},{160,96},{64,128},{224,160},{128,192},{32,2... | collective-permute-start | bytes 786440 | tf_op jit(solution)/shard_map/ppermute | solution.py:267
  10.1 0.0 collective-permute-start.2
  10.1 0.2 factors_1.1
  10.2 3.6 %collective-permute-start = (bf16[384,128]{1,0:T(8,128)(2,1)S(1)}, bf16[384,128]{1,0:T(8,128)(2,1)S(1)}, u32[]{:S(2)}, u32[]{:S(2)}) collective-permute-start(bf16[384,128]{1,0:T(8,128)(2,1)S(1)} %get-tuple-element.24), channel_id=1, source_target_pairs={{0,2},{2,0},{1,3},{3,1},{4,6},{6,4},{5,7},{7,5},{8,10},{10,8},{9,1... | collective-permute-start | bytes 294920 | tf_op jit(solution)/shard_map/ppermute | solution.py:262
  13.8 2.3 %collective-permute-done.got = bf16[384,128]{1,0:T(8,128)(2,1)S(1)} collective-permute-done((bf16[384,128]{1,0:T(8,128)(2,1)S(1)}, bf16[384,128]{1,0:T(8,128)(2,1)S(1)}, u32[]{:S(2)}, u32[]{:S(2)}) %collective-permute-start) | collective-permute-done | bytes 98336 | tf_op jit(solution)/shard_map/ppermute | solution.py:262
  16.1 4.2 %collective-permute-start.1 = (bf16[480,128]{1,0:T(8,128)(2,1)S(1)}, bf16[480,128]{1,0:T(8,128)(2,1)S(1)}, u32[]{:S(2)}, u32[]{:S(2)}) collective-permute-start(bf16[480,128]{1,0:T(8,128)(2,1)S(1)} %get-tuple-element.27), channel_id=1, source_target_pairs={{0,1},{1,0},{2,3},{3,2},{4,5},{5,4},{6,7},{7,6},{8,9},{9,8},{10,11... | collective-permute-start | bytes 368648 | tf_op jit(solution)/shard_map/ppermute | solution.py:262
  20.4 1.0 %collective-permute-done.1.got2 = bf16[480,128]{1,0:T(8,128)(2,1)S(1)} collective-permute-done((bf16[480,128]{1,0:T(8,128)(2,1)S(1)}, bf16[480,128]{1,0:T(8,128)(2,1)S(1)}, u32[]{:S(2)}, u32[]{:S(2)}) %collective-permute-start.1) | collective-permute-done | bytes 122912 | tf_op jit(solution)/shard_map/ppermute | solution.py:262
  21.3 0.8 %products.1 = (bf16[16,96,128]{2,1,0:T(8,128)(2,1)S(1)}, bf16[6,2048]{1,0:T(8,128)(2,1)}) custom-call(bf16[192,128]{1,0:T(8,128)(2,1)S(1)} %get-tuple-element.23.keep, bf16[384,128]{1,0:T(8,128)(2,1)S(1)} %collective-permute-done.got, f32[96,128]{1,0:T(8,128)S(1)} %get-tuple-element.26.half, bf16[480,128]{1,0:T(8,128)(2,1)S(1)} %collective-permute-done.1.got2), custom_call_target="tpu_custom_call" | custom-call | flops 100000000 | bytes 65536 | tf_op jit(solution)/shard_map/products/pallas_call | solution.py:327
  22.2 13.5 %conditional.1 = (bf16[16,96,128]{2,1,0:T(8,128)(2,1)S(1)}) conditional(s32[]{:T(128)} %convert_element_type.3, bf16[16,96,128]{2,1,0:T(8,128)(2,1)S(1)} %get-tuple-element.28, bf16[16,96,128]{2,1,0:T(8,128)(2,1)S(1)} %get-tuple-element.28), branch_computations={%region_0.0_spmd, %region_1.0_spmd} | conditional | bytes 1572872 | solution.py:341
  22.2 13.5 %all_to_all.9 = bf16[16,96,128]{2,1,0:T(8,128)(2,1)S(1)} all-to-all(bf16[16,96,128]{2,1,0:T(8,128)(2,1)S(1)} %copy.19), channel_id=1, replica_groups=mesh['zb'=4,'za'=2,'x'=4,'yl'=2,'yh'=2,'c'=2] {'yl','za','x'}, dimensions={0} | all-to-all | bytes 786432 | tf_op jit(solution)/shard_map/cond/branch_1_fun/all_to_all | solution.py:343
  35.7 0.0 collective-permute-done.4.refs_4_
  35.7 0.0 collective-permute-done.3.refs_3_
  35.7 0.0 collective-permute-done.2.refs_2_
  35.7 1.0 %inner.1 = bf16[64,16,128]{2,1,0:T(8,128)(2,1)S(1)} custom-call(bf16[16,96,128]{2,1,0:T(8,128)(2,1)S(1)} %get-tuple-element.31.refs_0_, bf16[64,2048]{1,0:T(8,128)(2,1)S(1)} %copy-done, bf16[64,2048]{1,0:T(8,128)(2,1)S(1)} %collective-permute-done.2.refs_2_, bf16[64,2048]{1,0:T(8,128)(2,1)S(1)} %collective-permute-done.3.refs_3_, ...), custom_call_target="tpu_custom_call" | custom-call | tf_op jit(solution)/shard_map/inner/pallas_call | solution.py:347
  36.7 16.0 %all_to_all.10.got = bf16[64,16,128]{2,1,0:T(8,128)(2,1)S(1)} all-to-all(bf16[64,16,128]{2,1,0:T(8,128)(2,1)S(1)} %inner.1), channel_id=1, replica_groups=mesh['zb'=4,'za'=2,'x'=4,'yl'=2,'yh'=2,'c'=2] {'yl','za','x','yh','c'}, dimensions={0} | all-to-all | bytes 524288 | tf_op jit(solution)/shard_map/all_to_all | solution.py:359
  52.7 0.9 %finish.1 = f32[6,4096]{1,0:T(8,128)} custom-call(bf16[64,16,128]{2,1,0:T(8,128)(2,1)S(1)} %all_to_all.10.got), custom_call_target="tpu_custom_call" | custom-call | tf_op jit(solution)/shard_map/finish/pallas_call | solution.py:360
  (2 shorter events, 0.0 us)
Async XLA Ops:
  0.6 4.3 %copy-start = (bf16[64,2048]{1,0:T(8,128)(2,1)S(1)}, bf16[64,2048]{1,0:T(8,128)(2,1)}, u32[]{:S(2)}) copy-start(bf16[64,2048]{1,0:T(8,128)(2,1)} %refs_1_.4) | copy-start | bytes 786436
  4.9 30.7 %collective-permute-start.4 = (bf16[64,2048]{1,0:T(8,128)(2,1)S(1)}, bf16[64,2048]{1,0:T(8,128)(2,1)S(1)}, u32[]{:S(2)}, u32[]{:S(2)}) collective-permute-start(bf16[64,2048]{1,0:T(8,128)(2,1)S(1)} %copy-done), channel_id=1, source_target_pairs={{160,0},{128,32},{224,64},{192,96},{32,128},{0,160},{96,192},{64,2... | collective-permute-start | bytes 786440 | tf_op jit(solution)/shard_map/ppermute | solution.py:267
  8.9 26.8 %collective-permute-start.3 = (bf16[64,2048]{1,0:T(8,128)(2,1)S(1)}, bf16[64,2048]{1,0:T(8,128)(2,1)S(1)}, u32[]{:S(2)}, u32[]{:S(2)}) collective-permute-start(bf16[64,2048]{1,0:T(8,128)(2,1)S(1)} %copy-done), channel_id=1, source_target_pairs={{192,0},{96,32},{0,64},{160,96},{64,128},{224,160},{128,192},{32,2... | collective-permute-start | bytes 786440 | tf_op jit(solution)/shard_map/ppermute | solution.py:267
  10.1 25.6 %collective-permute-start.2 = (bf16[64,2048]{1,0:T(8,128)(2,1)S(1)}, bf16[64,2048]{1,0:T(8,128)(2,1)S(1)}, u32[]{:S(2)}, u32[]{:S(2)}) collective-permute-start(bf16[64,2048]{1,0:T(8,128)(2,1)S(1)} %copy-done), channel_id=1, source_target_pairs={{224,0},{64,32},{32,64},{128,96},{96,128},{192,160},{160,192},{0,2... | collective-permute-start | bytes 786440 | tf_op jit(solution)/shard_map/ppermute | solution.py:267
  10.2 5.9 %collective-permute-start = (bf16[384,128]{1,0:T(8,128)(2,1)S(1)}, bf16[384,128]{1,0:T(8,128)(2,1)S(1)}, u32[]{:S(2)}, u32[]{:S(2)}) collective-permute-start(bf16[384,128]{1,0:T(8,128)(2,1)S(1)} %get-tuple-element.24), channel_id=1, source_target_pairs={{0,2},{2,0},{1,3},{3,1},{4,6},{6,4},{5,7},{7,5},{8,10},{10,8},{9,1... | collective-permute-start | bytes 294920 | tf_op jit(solution)/shard_map/ppermute | solution.py:262
  16.1 5.2 %collective-permute-start.1 = (bf16[480,128]{1,0:T(8,128)(2,1)S(1)}, bf16[480,128]{1,0:T(8,128)(2,1)S(1)}, u32[]{:S(2)}, u32[]{:S(2)}) collective-permute-start(bf16[480,128]{1,0:T(8,128)(2,1)S(1)} %get-tuple-element.27), channel_id=1, source_target_pairs={{0,1},{1,0},{2,3},{3,2},{4,5},{5,4},{6,7},{7,6},{8,9},{9,8},{10,11... | collective-permute-start | bytes 368648 | tf_op jit(solution)/shard_map/ppermute | solution.py:262

commit v9 on v8

--- a/solution.py
+++ b/solution.py
@@ -15,12 +15,13 @@
 GROUP = ("yl", "za", "x")
 PEERS = 16
 RING = 4
-ORDER = (0, 1, 2, 3)
+ORDER = (0, 2, 3, 1)
 EARLY_INPUT, EARLY_OUTPUT = 3, 2
 TILES = 2
 COUNT = 6
 OWN = 192
 HELD = 64
+HALF = HELD // 2
 KROWS = 16
 PART = COUNT * KROWS
 f32, bf16 = jnp.float32, jnp.bfloat16
@@ -308,18 +309,19 @@
 
     send, keep, own_sums = work(0)
     own, keep = lax.optimization_barrier((own, keep))
-    near = from_side(own, 1)
     middle = from_side(own, 2)
     far = from_side(own, 3)
-    held = (own, near, middle, far)
     send, keep, own_sums = work(1, send, keep, own_sums)
     got = swap(send, "yh")
+    late, keep = lax.optimization_barrier((own, keep))
+    near = [from_side(late[i * HALF : (i + 1) * HALF], 1) for i in range(2)]
+    held = (own, middle, far, *near)
     send2, half = pl.pallas_call(
         add_and_pack,
         out_shape=(shape((2 * OWN + PART, LANES), bf16), shape((PART, LANES), f32)),
         in_specs=[VMEM] * 3,
         out_specs=(VMEM, VMEM),
-        cost_estimate=pl.CostEstimate(flops=int(0.1e9), bytes_accessed=1 << 16, transcendentals=0),
+        cost_estimate=pl.CostEstimate(flops=int(1e9), bytes_accessed=1 << 10, transcendentals=0),
         compiler_params=params(4),
         name="add_and_pack",
     )(keep, own_sums, got)
@@ -333,7 +335,7 @@
             pltpu.VMEM((COUNT * SEQ, LANES), bf16),
             pltpu.VMEM((PART, LANES), f32),
         ],
-        cost_estimate=pl.CostEstimate(flops=int(0.1e9), bytes_accessed=1 << 16, transcendentals=0),
+        cost_estimate=pl.CostEstimate(flops=int(0.01e9), bytes_accessed=1 << 10, transcendentals=0),
         compiler_params=params(4),
         name="products",
     )(keep, got, half, got2)
@@ -347,7 +349,7 @@
     blocks = pl.pallas_call(
         inner,
         out_shape=shape((PEERS * 4, 8 * TILES, LANES), bf16),
-        in_specs=[VMEM] * 5,
+        in_specs=[VMEM] * 6,
         out_specs=VMEM,
         scratch_shapes=[
             pltpu.VMEM((PEERS * PART + 2 * KROWS, LANES), f32),

time: 54.2 us -> 53.9 us (level)
  the two profiles are of different devices: /device:TPU:1 before, /device:TPU:64 now
where the time goes in v9:
time: 53.9 us; the launch traced here: 53.8 us
  blocking collectives  31.3 us (58%)
  starting transfers between devices  11 us (20%)
  Pallas kernels  8.65 us (16%)
  waiting for transfers between devices  2.12 us (4%)
  between operations  0.71 us (1%)
    all_to_all x1, blocking collectives, on_device(): lax.all_to_all(v, GROUP, 0, 0, tiled=True)  15.9 us
    all_to_all x1, blocking collectives, on_device(): placed = lax.all_to_all(blocks, GROUP + TENSOR, 0, 0, tiled=True)  15.4 us
    ppermute x4, starting transfers between devices, from_side(): lax.ppermute(value, ('zb', 'za'), [((i + (distance if i % 2 else -distanc...  7.58 us
    pallas_call x2, Pallas kernels, work(): pl.pallas_call(functools.partial(factors, turn), out_shape=(pack, shape((...  5.92 us
    ppermute x2, starting transfers between devices, swap(): return lax.ppermute(value, axis, [(0, 1), (1, 0)])  3.38 us
    ppermute x2, waiting for transfers between devices, swap(): return lax.ppermute(value, axis, [(0, 1), (1, 0)])  2.11 us
  transfers between devices with their start and end apart: 6, of which 2 were waited for; matrix products, arithmetic and copies ran while one was open for 0% of the time, Pallas kernels for 8%

profile of v9, /device:TPU:64, one launch (start us, length us, event | category | flops | bytes accessed | tf_op | source)
XLA Modules:
  0.0 53.8 jit_solution(6965628364935072719)
XLA Ops:
  0.6 0.0 copy-start
  0.6 2.6 %factors_0.1 = (bf16[384,128]{1,0:T(8,128)(2,1)S(1)}, bf16[192,128]{1,0:T(8,128)(2,1)S(1)}, f32[192,128]{1,0:T(8,128)S(1)}) custom-call(bf16[768,1280]{1,0:T(8,128)(2,1)} %refs_0_.3, bf16[192,5120]{1,0:T(8,128)(2,1)} %refs_1_.3, bf16[1280,128]{1,0:T(8,128)(2,1)} %refs_2_.3, bf16[128,5120]{1,0:T(8,128)(2,1)} %refs_3_.3, f32[32,128]{1,0:T(8,128)} %bitcast.4, ...), custom_call_target="tpu_custom_call" | custom-call | flops 1000000000 | bytes 65536 | tf_op jit(solution)/shard_map/factors_0/pallas_call | solution.py:297
  3.2 0.0 copy-done
  3.2 3.3 %collective-permute-start.3 = (bf16[64,2048]{1,0:T(8,128)(2,1)S(1)}, bf16[64,2048]{1,0:T(8,128)(2,1)S(1)}, u32[]{:S(2)}, u32[]{:S(2)}) collective-permute-start(bf16[64,2048]{1,0:T(8,128)(2,1)S(1)} %copy-done), channel_id=1, source_target_pairs={{160,0},{128,32},{224,64},{192,96},{32,128},{0,160},{96,192},{64,2... | collective-permute-start | bytes 786440 | tf_op jit(solution)/shard_map/ppermute | solution.py:268
  6.5 2.2 %collective-permute-start.2 = (bf16[64,2048]{1,0:T(8,128)(2,1)S(1)}, bf16[64,2048]{1,0:T(8,128)(2,1)S(1)}, u32[]{:S(2)}, u32[]{:S(2)}) collective-permute-start(bf16[64,2048]{1,0:T(8,128)(2,1)S(1)} %copy-done), channel_id=1, source_target_pairs={{192,0},{96,32},{0,64},{160,96},{64,128},{224,160},{128,192},{32,2... | collective-permute-start | bytes 786440 | tf_op jit(solution)/shard_map/ppermute | solution.py:268
  8.7 3.3 %factors_1.1 = (bf16[384,128]{1,0:T(8,128)(2,1)S(1)}, bf16[192,128]{1,0:T(8,128)(2,1)S(1)}, f32[192,128]{1,0:T(8,128)S(1)}) custom-call(bf16[768,1280]{1,0:T(8,128)(2,1)} %refs_0_.3, bf16[192,5120]{1,0:T(8,128)(2,1)} %refs_1_.3, bf16[1280,128]{1,0:T(8,128)(2,1)} %refs_2_.3, ...), custom_call_target="tpu_custom_call", output_to_operand_aliasing={{0}: (8, {}), {1}: (9, {}), {2}: (10, {})} | custom-call | flops 1000000000 | bytes 65536 | tf_op jit(solution)/shard_map/factors_1/pallas_call | solution.py:297
  12.1 3.3 %collective-permute-start = (bf16[384,128]{1,0:T(8,128)(2,1)S(1)}, bf16[384,128]{1,0:T(8,128)(2,1)S(1)}, u32[]{:S(2)}, u32[]{:S(2)}) collective-permute-start(bf16[384,128]{1,0:T(8,128)(2,1)S(1)} %get-tuple-element.28), channel_id=1, source_target_pairs={{0,2},{2,0},{1,3},{3,1},{4,6},{6,4},{5,7},{7,5},{8,10},{10,8},{9,1... | collective-permute-start | bytes 294920 | tf_op jit(solution)/shard_map/ppermute | solution.py:263
  15.4 0.1 collective-permute-start.5
  15.5 2.0 %collective-permute-start.4 = (bf16[32,2048]{1,0:T(8,128)(2,1)S(1)}, bf16[32,2048]{1,0:T(8,128)(2,1)S(1)}, u32[]{:S(2)}, u32[]{:S(2)}) collective-permute-start(bf16[32,2048]{1,0:T(8,128)(2,1)S(1)} %get-tuple-element.36), channel_id=1, source_target_pairs={{224,0},{64,32},{32,64},{128,96},{96,128},{192,160},{160,192},{0,2... | collective-permute-start | bytes 393224 | tf_op jit(solution)/shard_map/ppermute | solution.py:268
  17.5 0.8 %collective-permute-done.got = bf16[384,128]{1,0:T(8,128)(2,1)S(1)} collective-permute-done((bf16[384,128]{1,0:T(8,128)(2,1)S(1)}, bf16[384,128]{1,0:T(8,128)(2,1)S(1)}, u32[]{:S(2)}, u32[]{:S(2)}) %collective-permute-start) | collective-permute-done | bytes 98336 | tf_op jit(solution)/shard_map/ppermute | solution.py:263
  18.3 0.1 collective-permute-start.1
  18.4 1.3 %collective-permute-done.1.got2 = bf16[480,128]{1,0:T(8,128)(2,1)S(1)} collective-permute-done((bf16[480,128]{1,0:T(8,128)(2,1)S(1)}, bf16[480,128]{1,0:T(8,128)(2,1)S(1)}, u32[]{:S(2)}, u32[]{:S(2)}) %collective-permute-start.1) | collective-permute-done | bytes 122912 | tf_op jit(solution)/shard_map/ppermute | solution.py:263
  19.7 0.8 %products.1 = (bf16[16,96,128]{2,1,0:T(8,128)(2,1)S(1)}, bf16[6,2048]{1,0:T(8,128)(2,1)}) custom-call(bf16[192,128]{1,0:T(8,128)(2,1)S(1)} %get-tuple-element.27.keep, bf16[384,128]{1,0:T(8,128)(2,1)S(1)} %collective-permute-done.got, f32[96,128]{1,0:T(8,128)S(1)} %get-tuple-element.30.half, bf16[480,128]{1,0:T(8,128)(2,1)S(1)} %collective-permute-done.1.got2), custom_call_target="tpu_custom_call" | custom-call | flops 10000000 | bytes 1024 | tf_op jit(solution)/shard_map/products/pallas_call | solution.py:329
  20.6 15.9 %conditional.1 = (bf16[16,96,128]{2,1,0:T(8,128)(2,1)S(1)}) conditional(s32[]{:T(128)} %convert_element_type.3, bf16[16,96,128]{2,1,0:T(8,128)(2,1)S(1)} %get-tuple-element.32, bf16[16,96,128]{2,1,0:T(8,128)(2,1)S(1)} %get-tuple-element.32), branch_computations={%region_0.0_spmd, %region_1.0_spmd} | conditional | bytes 1572872 | solution.py:343
  20.6 15.9 %all_to_all.9 = bf16[16,96,128]{2,1,0:T(8,128)(2,1)S(1)} all-to-all(bf16[16,96,128]{2,1,0:T(8,128)(2,1)S(1)} %copy.19), channel_id=1, replica_groups=mesh['zb'=4,'za'=2,'x'=4,'yl'=2,'yh'=2,'c'=2] {'yl','za','x'}, dimensions={0} | all-to-all | bytes 786432 | tf_op jit(solution)/shard_map/cond/branch_1_fun/all_to_all | solution.py:345
  36.5 0.0 collective-permute-done.5.refs_5_
  36.5 0.0 collective-permute-done.4.refs_4_
  36.5 0.0 collective-permute-done.3.refs_3_
  36.5 0.0 collective-permute-done.2.refs_2_
  36.5 1.0 %inner.1 = bf16[64,16,128]{2,1,0:T(8,128)(2,1)S(1)} custom-call(bf16[16,96,128]{2,1,0:T(8,128)(2,1)S(1)} %get-tuple-element.37.refs_0_, bf16[64,2048]{1,0:T(8,128)(2,1)S(1)} %copy-done, bf16[64,2048]{1,0:T(8,128)(2,1)S(1)} %collective-permute-done.2.refs_2_, bf16[64,2048]{1,0:T(8,128)(2,1)S(1)} %collective-permute-done.3.refs_3_, ...), custom_call_target="tpu_custom_call" | custom-call | tf_op jit(solution)/shard_map/inner/pallas_call | solution.py:349
  37.5 15.4 %all_to_all.10.got = bf16[64,16,128]{2,1,0:T(8,128)(2,1)S(1)} all-to-all(bf16[64,16,128]{2,1,0:T(8,128)(2,1)S(1)} %inner.1), channel_id=1, replica_groups=mesh['zb'=4,'za'=2,'x'=4,'yl'=2,'yh'=2,'c'=2] {'yl','za','x','yh','c'}, dimensions={0} | all-to-all | bytes 524288 | tf_op jit(solution)/shard_map/all_to_all | solution.py:361
  52.9 0.9 %finish.1 = f32[6,4096]{1,0:T(8,128)} custom-call(bf16[64,16,128]{2,1,0:T(8,128)(2,1)S(1)} %all_to_all.10.got), custom_call_target="tpu_custom_call" | custom-call | tf_op jit(solution)/shard_map/finish/pallas_call | solution.py:362
  (3 shorter events, 0.1 us)
Async XLA Ops:
  0.6 2.6 %copy-start = (bf16[64,2048]{1,0:T(8,128)(2,1)S(1)}, bf16[64,2048]{1,0:T(8,128)(2,1)}, u32[]{:S(2)}) copy-start(bf16[64,2048]{1,0:T(8,128)(2,1)} %refs_1_.4) | copy-start | bytes 786436
  3.2 33.3 %collective-permute-start.3 = (bf16[64,2048]{1,0:T(8,128)(2,1)S(1)}, bf16[64,2048]{1,0:T(8,128)(2,1)S(1)}, u32[]{:S(2)}, u32[]{:S(2)}) collective-permute-start(bf16[64,2048]{1,0:T(8,128)(2,1)S(1)} %copy-done), channel_id=1, source_target_pairs={{160,0},{128,32},{224,64},{192,96},{32,128},{0,160},{96,192},{64,2... | collective-permute-start | bytes 786440 | tf_op jit(solution)/shard_map/ppermute | solution.py:268
  6.5 30.0 %collective-permute-start.2 = (bf16[64,2048]{1,0:T(8,128)(2,1)S(1)}, bf16[64,2048]{1,0:T(8,128)(2,1)S(1)}, u32[]{:S(2)}, u32[]{:S(2)}) collective-permute-start(bf16[64,2048]{1,0:T(8,128)(2,1)S(1)} %copy-done), channel_id=1, source_target_pairs={{192,0},{96,32},{0,64},{160,96},{64,128},{224,160},{128,192},{32,2... | collective-permute-start | bytes 786440 | tf_op jit(solution)/shard_map/ppermute | solution.py:268
  12.1 6.2 %collective-permute-start = (bf16[384,128]{1,0:T(8,128)(2,1)S(1)}, bf16[384,128]{1,0:T(8,128)(2,1)S(1)}, u32[]{:S(2)}, u32[]{:S(2)}) collective-permute-start(bf16[384,128]{1,0:T(8,128)(2,1)S(1)} %get-tuple-element.28), channel_id=1, source_target_pairs={{0,2},{2,0},{1,3},{3,1},{4,6},{6,4},{5,7},{7,5},{8,10},{10,8},{9,1... | collective-permute-start | bytes 294920 | tf_op jit(solution)/shard_map/ppermute | solution.py:263
  15.4 21.1 %collective-permute-start.5 = (bf16[32,2048]{1,0:T(8,128)(2,1)S(1)}, bf16[32,2048]{1,0:T(8,128)(2,1)S(1)}, u32[]{:S(2)}, u32[]{:S(2)}) collective-permute-start(bf16[32,2048]{1,0:T(8,128)(2,1)S(1)} %get-tuple-element.35), channel_id=1, source_target_pairs={{224,0},{64,32},{32,64},{128,96},{96,128},{192,160},{160,192},{0,2... | collective-permute-start | bytes 393224 | tf_op jit(solution)/shard_map/ppermute | solution.py:268
  15.5 21.0 %collective-permute-start.4 = (bf16[32,2048]{1,0:T(8,128)(2,1)S(1)}, bf16[32,2048]{1,0:T(8,128)(2,1)S(1)}, u32[]{:S(2)}, u32[]{:S(2)}) collective-permute-start(bf16[32,2048]{1,0:T(8,128)(2,1)S(1)} %get-tuple-element.36), channel_id=1, source_target_pairs={{224,0},{64,32},{32,64},{128,96},{96,128},{192,160},{160,192},{0,2... | collective-permute-start | bytes 393224 | tf_op jit(solution)/shard_map/ppermute | solution.py:268
  18.3 1.4 %collective-permute-start.1 = (bf16[480,128]{1,0:T(8,128)(2,1)S(1)}, bf16[480,128]{1,0:T(8,128)(2,1)S(1)}, u32[]{:S(2)}, u32[]{:S(2)}) collective-permute-start(bf16[480,128]{1,0:T(8,128)(2,1)S(1)} %get-tuple-element.31), channel_id=1, source_target_pairs={{0,1},{1,0},{2,3},{3,2},{4,5},{5,4},{6,7},{7,6},{8,9},{9,8},{10,11... | collective-permute-start | bytes 368648 | tf_op jit(solution)/shard_map/ppermute | solution.py:263
